TPU v7x, 512 devices: a whole 4x4x16 slice. The times are simulated.
512 devices in a mesh: ctx: 16 (over y, x), sp: 32 (over z, core).
Axes of the slice: x: 4, y: 4, z: 16, core: 2. Of those that a mesh axis runs over, the one named last changes fastest.
Arguments:
- query_rows: bfloat16 [65536, 2048], P(('ctx', 'sp')), may hold values from -6 to 6
- key_rows: bfloat16 [65536, 2048], P(('ctx', 'sp')), may hold values from -6 to 6
- value_rows: bfloat16 [65536, 2048], P(('ctx', 'sp')), may hold values from -6 to 6
- out_grad: bfloat16 [65536, 2048], P(('ctx', 'sp')), may hold values from -6 to 6
- positions: int32 [65536], P(('ctx', 'sp')), may hold values from 0 to 4095, as said below
Outputs:
- query_grad: bfloat16 [65536, 2048], P(('ctx', 'sp'))
- key_grad: bfloat16 [65536, 2048], P(('ctx', 'sp'))
- value_grad: bfloat16 [65536, 2048], P(('ctx', 'sp'))
Inputs may be any that keep to these rules, and one draw needn't show every extreme that they name: `positions`: each token's position within its document, 0 at a document's first token and rising by one per token; a document starts at least at the first token of every group of 128 * 32 consecutive tokens, and the first such group is one whole document.
All inputs are finite; a program needn't handle non-finite values.
Results may differ from a plain program's by a relative error of at most 0.0063.
Values may be sent and summed in bfloat16 or wider, within the bound.
No kernel may reach another device: no remote copies, remote signals or barrier semaphores. Data moves between devices by JAX's collectives and lax.ppermute only.
A program may use at most 64 MiB of HBM per device.

v0:
```python
import functools
import math

import jax
import jax.numpy as jnp
import numpy as np
from jax import lax
from jax.experimental import pallas as pl
from jax.experimental.pallas import tpu as pltpu
from jax.sharding import Mesh, PartitionSpec as P

HD = 64
SPAN = 128
BASE = 500000.0
PAIR = 2 * HD
F32 = jnp.float32
BF16 = jnp.bfloat16
STEP = 4
VMEM_LIMIT = 40 * 1024 * 1024

NT = (((1,), (1,)), ((), ()))
TN = (((0,), (0,)), ((), ()))
NN = (((1,), (0,)), ((), ()))


def dot(a, b, dims):
    return lax.dot_general(a, b, dims, preferred_element_type=F32)


def lanes(rows):
    return lax.broadcasted_iota(jnp.int32, (rows, PAIR), 1)


def swap_halves(x):
    first = (lanes(x.shape[0]) % HD) < HD // 2
    return jnp.where(first, pltpu.roll(x, PAIR - HD // 2, 1), pltpu.roll(x, HD // 2, 1))


def rotated(x, cosine, sine):
    x = x.astype(F32)
    return x * cosine + swap_halves(x) * sine


def by_head(x):
    first = lanes(x.shape[0]) < HD
    zero = jnp.zeros_like(x)
    return jnp.concatenate([jnp.where(first, x, zero), jnp.where(first, zero, x)], axis=0)


def pack_pair(m):
    first = lanes(HD) < HD
    return jnp.where(first, m[:HD], m[HD:])


def states_kernel(q_ref, k_ref, v_ref, g_ref, cos_ref, sin_ref, qr_ref, kr_ref, st_ref):
    cosine, sine = cos_ref[...], sin_ref[...]
    for p in range(STEP):
        at = slice(p * PAIR, (p + 1) * PAIR)
        q = rotated(q_ref[:, at], cosine, sine).astype(BF16)
        k = rotated(k_ref[:, at], cosine, sine).astype(BF16)
        qr_ref[:, at] = q
        kr_ref[:, at] = k
        state = pack_pair(dot(k, v_ref[:, at], TN)).astype(BF16)
        grad = pack_pair(dot(q, g_ref[:, at], TN)).astype(BF16)
        for r in range(2):
            st_ref[0, 2 * p + r, 0] = state[32 * r : 32 * r + 32]
            st_ref[0, 2 * p + r, 1] = grad[32 * r : 32 * r + 32]


def block_kernel(q_ref, k_ref, v_ref, g_ref, qo_ref, ko_ref, vo_ref):
    row = lax.broadcasted_iota(jnp.int32, (SPAN, 2 * SPAN), 0)
    col = lax.broadcasted_iota(jnp.int32, (SPAN, 2 * SPAN), 1) % SPAN
    lower = row >= col
    upper = row <= col
    for p in range(STEP):
        at = slice(p * PAIR, (p + 1) * PAIR)
        q, k, v, g = q_ref[:, at], k_ref[:, at], v_ref[:, at], g_ref[:, at]
        q2, k2, v2, g2 = by_head(q), by_head(k), by_head(v), by_head(g)
        w = jnp.where(lower, dot(g, v2, NT), 0.0).astype(BF16)
        wt = jnp.where(upper, dot(v, g2, NT), 0.0).astype(BF16)
        st = jnp.where(upper, dot(k, q2, NT), 0.0).astype(BF16)
        qo_ref[:, at] = dot(w, k2, NN)
        ko_ref[:, at] = dot(wt, q2, NN)
        vo_ref[:, at] = dot(st, g2, NN)


def finish_kernel(
    factor, k_ref, v_ref, g_ref, cos_ref, sin_ref, st_ref, qi_ref, ki_ref, vi_ref, qo_ref, ko_ref, vo_ref
):
    cosine, sine = cos_ref[...], -sin_ref[...]
    for p in range(STEP):
        at = slice(p * PAIR, (p + 1) * PAIR)
        k, v, g = k_ref[:, at], v_ref[:, at], g_ref[:, at]
        before = by_head(jnp.concatenate([st_ref[0, 2 * p, 0], st_ref[0, 2 * p + 1, 0]], axis=0))
        after = by_head(jnp.concatenate([st_ref[0, 2 * p, 1], st_ref[0, 2 * p + 1, 1]], axis=0))
        qo = (factor * (qi_ref[:, at] + dot(g, before, NT))).astype(BF16)
        ko = (factor * (ki_ref[:, at] + dot(v, after, NT))).astype(BF16)
        vo_ref[:, at] = (factor * (vi_ref[:, at] + dot(k, after, NN))).astype(BF16)
        qo_ref[:, at] = rotated(qo, cosine, sine).astype(BF16)
        ko_ref[:, at] = rotated(ko, cosine, sine).astype(BF16)


def totals_kernel(zr_ref, out_ref):
    state = zr_ref[0, 0].astype(F32)
    grad = zr_ref[0, 1].astype(F32)
    for z in range(1, zr_ref.shape[0]):
        state += zr_ref[z, 0].astype(F32)
        grad += zr_ref[z, 1].astype(F32)
    me = lax.axis_index("ctx")
    for j in range(out_ref.shape[0]):
        out_ref[j] = jnp.where(j > me, state, grad)


def scan_kernel(zr_ref, cx_ref, out_ref):
    me = lax.axis_index("ctx")
    state = jnp.zeros(cx_ref.shape[1:], F32)
    grad = jnp.zeros(cx_ref.shape[1:], F32)
    for j in range(cx_ref.shape[0]):
        state += jnp.where(j < me, cx_ref[j], 0.0)
        grad += jnp.where(j > me, cx_ref[j], 0.0)
    count = zr_ref.shape[0]
    for z in range(count):
        out_ref[z, 0] = state.astype(BF16)
        state += zr_ref[z, 0].astype(F32)
    for z in reversed(range(count)):
        out_ref[z, 1] = grad.astype(BF16)
        grad += zr_ref[z, 1].astype(F32)


def pair_sum_kernel(cc_ref, out_ref):
    for z in range(out_ref.shape[0]):
        out_ref[z] = (cc_ref[0, z].astype(F32) + cc_ref[1, z].astype(F32)).astype(BF16)


def spread_kernel(zb_ref, cc_ref, out_ref):
    for z in range(zb_ref.shape[0]):
        state, grad = zb_ref[z, 0], zb_ref[z, 1]
        out_ref[0, z, 0] = state
        out_ref[1, z, 0] = (state.astype(F32) + cc_ref[0, z, 0].astype(F32)).astype(BF16)
        out_ref[0, z, 1] = (grad.astype(F32) + cc_ref[1, z, 1].astype(F32)).astype(BF16)
        out_ref[1, z, 1] = grad


def whole(kernel, out_shape, *args):
    spec = pl.BlockSpec(memory_space=pltpu.VMEM)
    return pl.pallas_call(
        kernel,
        out_shape=out_shape,
        in_specs=[spec] * len(args),
        out_specs=spec,
        compiler_params=pltpu.CompilerParams(vmem_limit_bytes=VMEM_LIMIT),
    )(*args)


def on_device(query_rows, key_rows, value_rows, out_grad, positions):
    tokens, width = query_rows.shape
    n_ctx, n_z = lax.axis_size("ctx"), lax.axis_size("z")
    seq_total = tokens * n_ctx * n_z * lax.axis_size("core")
    factor = 1.0 / math.sqrt(HD * seq_total)
    half = HD // 2
    frequency = BASE ** (-jnp.arange(half, dtype=F32) / half)
    frequency = jnp.tile(frequency, PAIR // half)
    sign = jnp.asarray(np.tile(np.repeat(np.float32([-1.0, 1.0]), half), 2))
    angles = positions.astype(F32)[:, None] * frequency[None, :]
    cosine, sine = jnp.cos(angles), jnp.sin(angles) * sign[None, :]

    pairs = width // PAIR
    steps = pairs // STEP
    slots = 2 * pairs // 2
    rows = pl.BlockSpec((tokens, STEP * PAIR), lambda i: (0, i))
    table = pl.BlockSpec((tokens, PAIR), lambda i: (0, 0))
    per_half = steps // 2
    chunk = pl.BlockSpec((1, 2 * STEP, 2, HD // 2, PAIR), lambda i: (i // per_half, i % per_half, 0, 0, 0))
    params = pltpu.CompilerParams(vmem_limit_bytes=VMEM_LIMIT, dimension_semantics=("arbitrary",))
    like = jax.ShapeDtypeStruct((tokens, width), BF16)
    wide = jax.ShapeDtypeStruct((tokens, width), F32)
    states_shape = jax.ShapeDtypeStruct((2, slots, 2, HD // 2, PAIR), BF16)
    half_shape = jax.ShapeDtypeStruct((slots, 2, HD // 2, PAIR), BF16)

    query, key, states = pl.pallas_call(
        states_kernel,
        grid=(steps,),
        in_specs=[rows] * 4 + [table] * 2,
        out_specs=[rows, rows, chunk],
        out_shape=[like, like, states_shape],
        compiler_params=params,
    )(query_rows, key_rows, value_rows, out_grad, cosine, sine)

    cores = lax.all_to_all(states, "core", 0, 0, tiled=True)
    chip = whole(pair_sum_kernel, half_shape, cores)
    over_z = lax.all_to_all(chip, "z", 0, 0, tiled=True)

    flops = 12 * 2 * SPAN**3 * pairs
    query_in, key_in, value_in = pl.pallas_call(
        block_kernel,
        grid=(steps,),
        in_specs=[rows] * 4,
        out_specs=[rows] * 3,
        out_shape=[wide] * 3,
        compiler_params=params,
        cost_estimate=pl.CostEstimate(flops=flops, bytes_accessed=5 * 2**20, transcendentals=0),
    )(query, key, value_rows, out_grad)

    group = whole(
        totals_kernel, jax.ShapeDtypeStruct((n_ctx, HD // 2, PAIR), F32), over_z
    )
    over_ctx = lax.all_to_all(group, "ctx", 0, 0, tiled=True)
    sums = whole(scan_kernel, half_shape, over_z, over_ctx)
    back = lax.all_to_all(sums, "z", 0, 0, tiled=True)
    spread = whole(spread_kernel, states_shape, back, cores)
    carried = lax.all_to_all(spread, "core", 0, 0, tiled=True)

    return pl.pallas_call(
        functools.partial(finish_kernel, factor),
        grid=(steps,),
        in_specs=[rows] * 3 + [table] * 2 + [chunk] + [rows] * 3,
        out_specs=[rows] * 3,
        out_shape=[like] * 3,
        compiler_params=params,
    )(key, value_rows, out_grad, cosine, sine, carried, query_in, key_in, value_in)


def solution(mesh):
    split = Mesh(
        mesh.devices.reshape(mesh.shape["ctx"], mesh.shape["sp"] // 2, 2), ("ctx", "z", "core")
    )
    tokens = ("ctx", "z", "core")
    return jax.shard_map(
        on_device,
        mesh=split,
        in_specs=(P(tokens, None),) * 4 + (P(tokens),),
        out_specs=(P(tokens, None),) * 3,
        check_vma=False,
    )
```

profile of v0, /device:TPU:1, one launch (start us, length us, event | category | flops | bytes accessed | tf_op | source)
XLA Modules:
  0.0 94.6 jit_solution(6967792196551153447)
XLA Ops:
  0.6 0.0 copy-start.13
  0.7 0.6 copy-done.13
  1.3 0.1 mul.24
  1.4 0.6 copy-done.12
  1.9 0.3 fusion
  2.3 0.0 copy-start
  2.3 1.0 %copy-done = bf16[128,2048]{1,0:T(8,128)(2,1)S(1)} copy-done((bf16[128,2048]{1,0:T(8,128)(2,1)S(1)}, bf16[128,2048]{1,0:T(8,128)(2,1)}, u32[]{:S(2)}) %copy-start) | copy-done | bytes 524312
  3.3 1.0 %copy-done.2 = bf16[128,2048]{1,0:T(8,128)(2,1)S(1)} copy-done((bf16[128,2048]{1,0:T(8,128)(2,1)S(1)}, bf16[128,2048]{1,0:T(8,128)(2,1)}, u32[]{:S(2)}) %copy-start.2) | copy-done | bytes 524312
  4.3 1.0 %copy-done.8 = bf16[128,2048]{1,0:T(8,128)(2,1)S(1)} copy-done((bf16[128,2048]{1,0:T(8,128)(2,1)S(1)}, bf16[128,2048]{1,0:T(8,128)(2,1)}, u32[]{:S(2)}) %copy-start.8) | copy-done | bytes 524312
  5.4 1.0 %copy-done.9 = bf16[128,2048]{1,0:T(8,128)(2,1)S(1)} copy-done((bf16[128,2048]{1,0:T(8,128)(2,1)S(1)}, bf16[128,2048]{1,0:T(8,128)(2,1)}, u32[]{:S(2)}) %copy-start.9) | copy-done | bytes 524312
  6.4 2.0 %shard_map.85 = (bf16[128,2048]{1,0:T(8,128)(2,1)S(1)}, bf16[128,2048]{1,0:T(8,128)(2,1)S(1)}, bf16[2,16,2,32,128]{4,3,2,1,0:T(8,128)(2,1)S(1)}) custom-call(bf16[128,2048]{1,0:T(8,128)(2,1)S(1)} %copy-done.8, bf16[128,2048]{1,0:T(8,128)(2,1)S(1)} %copy-done.9, bf16[128,2048]{1,0:T(8,128)(2,1)S(1)} %copy-done, bf16[128,2048]{1,0:T(8,128)(2,1)S(1)} %copy-done.2, ...), custom_call_target="tpu_custom_call" | custom-call | tf_op jit(solution)/shard_map/pallas_call | solution.py:180
  8.5 0.0 copy-start.10
  8.5 10.7 %all_to_all.25.cc_ref = bf16[2,16,2,32,128]{4,3,2,1,0:T(8,128)(2,1)S(1)} all-to-all(bf16[2,16,2,32,128]{4,3,2,1,0:T(8,128)(2,1)S(1)} %get-tuple-element.10), channel_id=1, replica_groups=mesh['ctx'=16,'z'=16,'core'=2] {'core'}, dimensions={0} | all-to-all | bytes 1048576 | tf_op jit(solution)/shard_map/all_to_all | solution.py:189
  19.2 0.0 copy-done.10
  19.2 0.1 shard_map.86
  19.2 23.4 %all_to_all.26.zr_ref = bf16[16,2,32,128]{3,2,1,0:T(8,128)(2,1)S(1)} all-to-all(bf16[16,2,32,128]{3,2,1,0:T(8,128)(2,1)S(1)} %shard_map.86), channel_id=1, replica_groups=mesh['ctx'=16,'z'=16,'core'=2] {'z'}, dimensions={0} | all-to-all | bytes 524288 | tf_op jit(solution)/shard_map/all_to_all | solution.py:191
  42.6 0.1 shard_map.87
  42.6 14.1 %all_to_all.27.cx_ref = f32[16,32,128]{2,1,0:T(8,128)S(1)} all-to-all(f32[16,32,128]{2,1,0:T(8,128)S(1)} %shard_map.87), channel_id=1, replica_groups=mesh['ctx'=16,'z'=16,'core'=2] {'ctx'}, dimensions={0} | all-to-all | bytes 524288 | tf_op jit(solution)/shard_map/all_to_all | solution.py:207
  56.7 0.8 shard_map.88
  57.5 10.2 %all-to-all-start.3 = ((bf16[16,2,32,128]{3,2,1,0:T(8,128)(2,1)}), bf16[16,2,32,128]{3,2,1,0:T(8,128)(2,1)S(1)}, u32[]{:S(2)}, u32[]{:S(2)}) async-start(bf16[16,2,32,128]{3,2,1,0:T(8,128)(2,1)} %shard_map.88), calls=%async_computation.3 | async-start | bytes 524288 | tf_op jit(solution)/shard_map/all_to_all | solution.py:209
  67.8 0.0 copy-done.1
  67.8 0.0 copy-done.3
  67.8 0.0 copy-start.11
  67.8 1.0 %copy-done.11 = bf16[128,2048]{1,0:T(8,128)(2,1)S(1)} copy-done((bf16[128,2048]{1,0:T(8,128)(2,1)S(1)}, bf16[128,2048]{1,0:T(8,128)(2,1)}, u32[]{:S(2)}) %copy-start.11) | copy-done | bytes 524312
  68.8 4.0 %shard_map.90 = (f32[128,2048]{1,0:T(8,128)S(1)}, f32[128,2048]{1,0:T(8,128)S(1)}, f32[128,2048]{1,0:T(8,128)S(1)}) custom-call(bf16[128,2048]{1,0:T(8,128)(2,1)S(1)} %copy-done.11, bf16[128,2048]{1,0:T(8,128)(2,1)S(1)} %get-tuple-element.9.k_ref, bf16[128,2048]{1,0:T(8,128)(2,1)S(1)} %copy-done.1, bf16[128,2048]{1,0:T(8,128)(2,1)S(1)} %copy-done.3), custom_call_target="tpu_custom_call" | custom-call | flops 805306368 | bytes 5242880 | tf_op jit(solution)/shard_map/pallas_call | solution.py:194
  72.8 0.0 copy-start.4
  72.8 1.0 %copy-done.4 = f32[128,2048]{1,0:T(8,128)} copy-done((f32[128,2048]{1,0:T(8,128)}, f32[128,2048]{1,0:T(8,128)S(1)}, u32[]{:S(2)}) %copy-start.4) | copy-done | bytes 1048600
  73.8 1.0 %copy-done.6 = f32[128,2048]{1,0:T(8,128)} copy-done((f32[128,2048]{1,0:T(8,128)}, f32[128,2048]{1,0:T(8,128)S(1)}, u32[]{:S(2)}) %copy-start.6) | copy-done | bytes 1048600
  74.8 5.8 %all-to-all-done.3.zb_ref = bf16[16,2,32,128]{3,2,1,0:T(8,128)(2,1)S(1)} async-done(((bf16[16,2,32,128]{3,2,1,0:T(8,128)(2,1)}), bf16[16,2,32,128]{3,2,1,0:T(8,128)(2,1)S(1)}, u32[]{:S(2)}, u32[]{:S(2)}) %all-to-all-start.3) | async-done | bytes 262176 | tf_op jit(solution)/shard_map/all_to_all | solution.py:209
  80.5 0.1 shard_map.89
  80.6 10.8 %all_to_all.28.st_ref = bf16[2,16,2,32,128]{4,3,2,1,0:T(8,128)(2,1)S(1)} all-to-all(bf16[2,16,2,32,128]{4,3,2,1,0:T(8,128)(2,1)S(1)} %shard_map.89), channel_id=1, replica_groups=mesh['ctx'=16,'z'=16,'core'=2] {'core'}, dimensions={0} | all-to-all | bytes 1048576 | tf_op jit(solution)/shard_map/all_to_all | solution.py:211
  91.4 3.2 %shard_map.91 = (bf16[128,2048]{1,0:T(8,128)(2,1)}, bf16[128,2048]{1,0:T(8,128)(2,1)}, bf16[128,2048]{1,0:T(8,128)(2,1)}) custom-call(bf16[128,2048]{1,0:T(8,128)(2,1)S(1)} %get-tuple-element.9.k_ref, bf16[128,2048]{1,0:T(8,128)(2,1)S(1)} %copy-done.1, bf16[128,2048]{1,0:T(8,128)(2,1)S(1)} %copy-done.3, f32[128,128]{1,0:T(8,128)S(1)} %get-tuple-element.16.cos_ref, ...), custom_call_target="tpu_custom_call" | custom-call | tf_op jit(solution)/shard_map/pallas_call | solution.py:213
  (14 shorter events, 0.0 us)
Async XLA Ops:
  0.6 0.7 copy-start.13
  1.3 0.7 copy-start.12
  2.3 1.0 %copy-start = (bf16[128,2048]{1,0:T(8,128)(2,1)S(1)}, bf16[128,2048]{1,0:T(8,128)(2,1)}, u32[]{:S(2)}) copy-start(bf16[128,2048]{1,0:T(8,128)(2,1)} %v_ref.5) | copy-start | bytes 1572868
  3.3 1.0 %copy-start.2 = (bf16[128,2048]{1,0:T(8,128)(2,1)S(1)}, bf16[128,2048]{1,0:T(8,128)(2,1)}, u32[]{:S(2)}) copy-start(bf16[128,2048]{1,0:T(8,128)(2,1)} %g_ref.5) | copy-start | bytes 1572868
  4.3 1.0 %copy-start.8 = (bf16[128,2048]{1,0:T(8,128)(2,1)S(1)}, bf16[128,2048]{1,0:T(8,128)(2,1)}, u32[]{:S(2)}) copy-start(bf16[128,2048]{1,0:T(8,128)(2,1)} %q_ref.1) | copy-start | bytes 1572868
  5.4 1.0 %copy-start.9 = (bf16[128,2048]{1,0:T(8,128)(2,1)S(1)}, bf16[128,2048]{1,0:T(8,128)(2,1)}, u32[]{:S(2)}) copy-start(bf16[128,2048]{1,0:T(8,128)(2,1)} %k_ref.1) | copy-start | bytes 1572868
  8.5 10.7 %copy-start.10 = (bf16[128,2048]{1,0:T(8,128)(2,1)}, bf16[128,2048]{1,0:T(8,128)(2,1)S(1)}, u32[]{:S(2)}) copy-start(bf16[128,2048]{1,0:T(8,128)(2,1)S(1)} %get-tuple-element.11.q_ref) | copy-start | bytes 1572868
  56.7 11.0 %copy-start.1 = (bf16[128,2048]{1,0:T(8,128)(2,1)S(1)}, bf16[128,2048]{1,0:T(8,128)(2,1)}, u32[]{:S(2)}) copy-start(bf16[128,2048]{1,0:T(8,128)(2,1)} %v_ref.5) | copy-start | bytes 1572868
  56.7 11.0 %copy-start.3 = (bf16[128,2048]{1,0:T(8,128)(2,1)S(1)}, bf16[128,2048]{1,0:T(8,128)(2,1)}, u32[]{:S(2)}) copy-start(bf16[128,2048]{1,0:T(8,128)(2,1)} %g_ref.5) | copy-start | bytes 1572868
  57.5 23.0 %all-to-all-start.3 = ((bf16[16,2,32,128]{3,2,1,0:T(8,128)(2,1)}), bf16[16,2,32,128]{3,2,1,0:T(8,128)(2,1)S(1)}, u32[]{:S(2)}, u32[]{:S(2)}) async-start(bf16[16,2,32,128]{3,2,1,0:T(8,128)(2,1)} %shard_map.88), calls=%async_computation.3 | async-start | bytes 524288 | tf_op jit(solution)/shard_map/all_to_all | solution.py:209
  67.8 1.0 %copy-start.11 = (bf16[128,2048]{1,0:T(8,128)(2,1)S(1)}, bf16[128,2048]{1,0:T(8,128)(2,1)}, u32[]{:S(2)}) copy-start(bf16[128,2048]{1,0:T(8,128)(2,1)} %copy-done.10) | copy-start | bytes 1572868
  72.8 1.0 %copy-start.4 = (f32[128,2048]{1,0:T(8,128)}, f32[128,2048]{1,0:T(8,128)S(1)}, u32[]{:S(2)}) copy-start(f32[128,2048]{1,0:T(8,128)S(1)} %get-tuple-element.13.ki_ref) | copy-start | bytes 3145732
  73.8 1.0 %copy-start.6 = (f32[128,2048]{1,0:T(8,128)}, f32[128,2048]{1,0:T(8,128)S(1)}, u32[]{:S(2)}) copy-start(f32[128,2048]{1,0:T(8,128)S(1)} %get-tuple-element.14.vi_ref) | copy-start | bytes 3145732
  80.5 10.9 %copy-start.5 = (f32[128,2048]{1,0:T(8,128)S(1)}, f32[128,2048]{1,0:T(8,128)}, u32[]{:S(2)}) copy-start(f32[128,2048]{1,0:T(8,128)} %copy-done.4) | copy-start | bytes 3145732
  80.5 10.9 %copy-start.7 = (f32[128,2048]{1,0:T(8,128)S(1)}, f32[128,2048]{1,0:T(8,128)}, u32[]{:S(2)}) copy-start(f32[128,2048]{1,0:T(8,128)} %copy-done.6) | copy-start | bytes 3145732
where the time goes:
time: 95.2 us; the launch traced here: 94.6 us
  blocking collectives  58.9 us (62%)
  Pallas kernels  10.2 us (11%)
  starting transfers between devices  10.2 us (11%)
  local copies, waits for them, and re-layouts  8.48 us (9%)
  waiting for transfers between devices  5.77 us (6%)
    all_to_all x1, blocking collectives, on_device(): over_z = lax.all_to_all(chip, 'z', 0, 0, tiled=True)  23.4 us
    all_to_all x1, blocking collectives, on_device(): over_ctx = lax.all_to_all(group, 'ctx', 0, 0, tiled=True)  14.1 us
    all_to_all x1, blocking collectives, on_device(): carried = lax.all_to_all(spread, 'core', 0, 0, tiled=True)  10.8 us
    all_to_all x1, blocking collectives, on_device(): cores = lax.all_to_all(states, 'core', 0, 0, tiled=True)  10.7 us
    all_to_all x1, starting transfers between devices, on_device(): back = lax.all_to_all(sums, 'z', 0, 0, tiled=True)  10.2 us
    unnamed x28, local copies, waits for them, and re-layouts  8.39 us
    all_to_all x1, waiting for transfers between devices, on_device(): back = lax.all_to_all(sums, 'z', 0, 0, tiled=True)  5.77 us
    pallas_call x1, Pallas kernels, on_device(): pl.pallas_call(block_kernel, grid=(steps,), in_specs=[rows] * 4, out_spec...  3.95 us
  transfers between devices with their start and end apart: 1, of which 1 were waited for; matrix products, arithmetic and copies ran while one was open for 0% of the time, Pallas kernels for 4%

commit v1 on v0

v1 whole, which is shorter than its diff:
```python
import functools
import math

import jax
import jax.numpy as jnp
from jax import lax
from jax.experimental import pallas as pl
from jax.experimental.pallas import tpu as pltpu
from jax.sharding import Mesh, PartitionSpec as P

HD = 64
SPAN = 128
BASE = 500000.0
PAIR = 2 * HD
HALF = HD // 2
F32 = jnp.float32
BF16 = jnp.bfloat16
GROUP = 4
VMEM_LIMIT = 16 * 1024 * 1024

NT = (((1,), (1,)), ((), ()))
TN = (((0,), (0,)), ((), ()))
NN = (((1,), (0,)), ((), ()))


def dot(a, b, dims):
    return lax.dot_general(a, b, dims, preferred_element_type=F32)


def lanes(rows):
    return lax.broadcasted_iota(jnp.int32, (rows, PAIR), 1)


def swap_halves(x):
    first = (lanes(x.shape[0]) % HD) < HALF
    return jnp.where(first, pltpu.roll(x, PAIR - HALF, 1), pltpu.roll(x, HALF, 1))


def rotated(x, cosine, sine):
    x = x.astype(F32)
    return x * cosine + swap_halves(x) * sine


def by_head(x):
    first = lanes(x.shape[0]) < HD
    zero = jnp.zeros_like(x)
    return jnp.concatenate([jnp.where(first, x, zero), jnp.where(first, zero, x)], axis=0)


def pack_pair(m):
    first = lanes(HD) < HD
    return jnp.where(first, m[:HD], m[HD:])


def angle_tables(positions):
    lane = lanes(1) % HALF
    frequency = jnp.ones((1, PAIR), F32)
    for bit in range(HALF.bit_length() - 1):
        part = BASE ** (-(2.0**bit) / HALF)
        frequency = jnp.where((lane >> bit) % 2 == 1, frequency * part, frequency)
    tokens = positions.shape[1]
    angles = jnp.broadcast_to(positions.astype(F32), (tokens, tokens)).T * frequency
    sign = jnp.where(lanes(1) % HD < HALF, -1.0, 1.0)
    return jnp.cos(angles), jnp.sin(angles) * sign


def span(first, count=1):
    return pl.ds(pl.multiple_of(first * PAIR, PAIR), count * PAIR)


def states_kernel(
    pos_ref, q_in, k_in, v_in, g_in,
    qr_ref, kr_ref, v_ref, g_ref, cos_ref, sin_ref, theirs_ref, mine_ref,
    q_ref, k_ref, sems,
):
    pairs = q_ref.shape[1] // PAIR
    core = lax.axis_index("core")
    first = (1 - core) * (pairs // 2)
    sources = ((q_in, q_ref), (k_in, k_ref), (v_in, v_ref), (g_in, g_ref))

    def copies(group):
        at = span(lax.rem(first + group * GROUP, pairs), GROUP)
        return [
            pltpu.make_async_copy(src.at[:, at], dst.at[:, at], sems.at[group, i])
            for i, (src, dst) in enumerate(sources)
        ]

    for group in range(pairs // GROUP):
        for copy in copies(group):
            copy.start()
    cosine, sine = angle_tables(pos_ref[...])
    cos_ref[...] = cosine
    sin_ref[...] = sine
    for j in range(pairs):
        if j % GROUP == 0:
            for copy in copies(j // GROUP):
                copy.wait()
        at = span(lax.rem(first + j, pairs))
        q = rotated(q_ref[:, at], cosine, sine).astype(BF16)
        k = rotated(k_ref[:, at], cosine, sine).astype(BF16)
        qr_ref[:, at] = q
        kr_ref[:, at] = k
        state = pack_pair(dot(k, v_ref[:, at], TN))
        grad = pack_pair(dot(q, g_ref[:, at], TN))
        out, slot = (theirs_ref, 2 * j) if j < pairs // 2 else (mine_ref, 2 * j - pairs)
        for r in range(2):
            rows = slice(HALF * r, HALF * (r + 1))
            out[slot + r, 0] = state[rows].astype(out.dtype)
            out[slot + r, 1] = grad[rows].astype(out.dtype)


def block_kernel(q_ref, k_ref, v_ref, g_ref, qo_ref, ko_ref, vo_ref):
    row = lax.broadcasted_iota(jnp.int32, (SPAN, 2 * SPAN), 0)
    col = lax.broadcasted_iota(jnp.int32, (SPAN, 2 * SPAN), 1) % SPAN
    lower = row >= col
    upper = row <= col
    for p in range(q_ref.shape[1] // PAIR):
        at = slice(p * PAIR, (p + 1) * PAIR)
        q, k, v, g = q_ref[:, at], k_ref[:, at], v_ref[:, at], g_ref[:, at]
        q2, k2, v2, g2 = by_head(q), by_head(k), by_head(v), by_head(g)
        w = jnp.where(lower, dot(g, v2, NT), 0.0).astype(BF16)
        wt = jnp.where(upper, dot(v, g2, NT), 0.0).astype(BF16)
        st = jnp.where(upper, dot(k, q2, NT), 0.0).astype(BF16)
        qo_ref[:, at] = dot(w, k2, NN)
        ko_ref[:, at] = dot(wt, q2, NN)
        vo_ref[:, at] = dot(st, g2, NN)


def chip_kernel(mine_ref, theirs_ref, out_ref):
    other = 1 - lax.axis_index("core")
    for z in range(out_ref.shape[0]):
        out_ref[z] = (mine_ref[z] + theirs_ref[other, z].astype(F32)).astype(BF16)


def totals_kernel(zr_ref, out_ref):
    state = zr_ref[0, 0].astype(F32)
    grad = zr_ref[0, 1].astype(F32)
    for z in range(1, zr_ref.shape[0]):
        state += zr_ref[z, 0].astype(F32)
        grad += zr_ref[z, 1].astype(F32)
    me = lax.axis_index("ctx")
    for j in range(out_ref.shape[0]):
        out_ref[j] = jnp.where(j > me, state, grad)


def scan_kernel(zr_ref, cx_ref, out_ref):
    me = lax.axis_index("ctx")
    state = jnp.zeros(cx_ref.shape[1:], F32)
    grad = jnp.zeros(cx_ref.shape[1:], F32)
    for j in range(cx_ref.shape[0]):
        state += jnp.where(j < me, cx_ref[j], 0.0)
        grad += jnp.where(j > me, cx_ref[j], 0.0)
    count = zr_ref.shape[0]
    for z in range(count):
        out_ref[z, 0] = state.astype(BF16)
        state += zr_ref[z, 0].astype(F32)
    for z in reversed(range(count)):
        out_ref[z, 1] = grad.astype(BF16)
        grad += zr_ref[z, 1].astype(F32)


def send_kernel(zb_ref, mine_ref, out_ref):
    core = lax.axis_index("core")
    for z in range(zb_ref.shape[0]):
        out_ref[z, 0] = (zb_ref[z, 0].astype(F32) + jnp.where(core == 0, mine_ref[z, 0], 0.0)).astype(BF16)
        out_ref[z, 1] = (zb_ref[z, 1].astype(F32) + jnp.where(core == 1, mine_ref[z, 1], 0.0)).astype(BF16)


def finish_kernel(
    factor, k_ref, v_ref, g_ref, cos_ref, sin_ref, zb_ref, theirs_ref, sent_ref, qi_ref, ki_ref, vi_ref,
    q_out, k_out, v_out, qo_ref, ko_ref, vo_ref, sems,
):
    pairs = k_ref.shape[1] // PAIR
    core = lax.axis_index("core")
    other = 1 - core
    first = core * (pairs // 2)
    cosine, sine = cos_ref[...], -sin_ref[...]
    results = ((qo_ref, q_out), (ko_ref, k_out), (vo_ref, v_out))
    copies = []

    def carried(slot, kind):
        count = zb_ref.shape[0]
        if slot >= count:
            return sent_ref[other, slot - count, kind]
        near = theirs_ref[other, slot, kind].astype(F32)
        return (zb_ref[slot, kind].astype(F32) + jnp.where(core == 1 - kind, near, 0.0)).astype(BF16)

    for j in range(pairs):
        at = span(lax.rem(first + j, pairs))
        k, v, g = k_ref[:, at], v_ref[:, at], g_ref[:, at]
        before = by_head(jnp.concatenate([carried(2 * j, 0), carried(2 * j + 1, 0)], axis=0))
        after = by_head(jnp.concatenate([carried(2 * j, 1), carried(2 * j + 1, 1)], axis=0))
        qo = (factor * (qi_ref[:, at] + dot(g, before, NT))).astype(BF16)
        ko = (factor * (ki_ref[:, at] + dot(v, after, NT))).astype(BF16)
        vo_ref[:, at] = (factor * (vi_ref[:, at] + dot(k, after, NN))).astype(BF16)
        qo_ref[:, at] = rotated(qo, cosine, sine).astype(BF16)
        ko_ref[:, at] = rotated(ko, cosine, sine).astype(BF16)
        if j % GROUP == GROUP - 1:
            group = j // GROUP
            done = span(lax.rem(first + group * GROUP, pairs), GROUP)
            for i, (src, dst) in enumerate(results):
                copies.append(pltpu.make_async_copy(src.at[:, done], dst.at[:, done], sems.at[group, i]))
                copies[-1].start()
    for copy in copies:
        copy.wait()


VMEM = pl.BlockSpec(memory_space=pltpu.VMEM)
HBM = pl.BlockSpec(memory_space=pltpu.HBM)


def call(kernel, out_shape, *args, out_specs=VMEM, in_specs=None, scratch=(), flops=0):
    in_specs = in_specs or [VMEM] * len(args)
    args = [pltpu.with_memory_space_constraint(x, spec.memory_space) for x, spec in zip(args, in_specs)]
    placed = jax.tree.map(lambda spec, x: spec.memory_space(x.shape, x.dtype), out_specs, out_shape)
    return pl.pallas_call(
        kernel,
        out_shape=placed,
        in_specs=in_specs,
        out_specs=out_specs,
        scratch_shapes=scratch,
        compiler_params=pltpu.CompilerParams(vmem_limit_bytes=VMEM_LIMIT),
        cost_estimate=pl.CostEstimate(flops=flops, bytes_accessed=2**20, transcendentals=0),
    )(*args)


def on_device(query_rows, key_rows, value_rows, out_grad, positions):
    tokens, width = query_rows.shape
    n_ctx, n_z = lax.axis_size("ctx"), lax.axis_size("z")
    seq_total = tokens * n_ctx * n_z * lax.axis_size("core")
    factor = 1.0 / math.sqrt(HD * seq_total)
    pairs = width // PAIR
    groups = pairs // GROUP
    like = jax.ShapeDtypeStruct((tokens, width), BF16)
    wide = jax.ShapeDtypeStruct((tokens, width), F32)
    table = jax.ShapeDtypeStruct((tokens, PAIR), F32)
    half_low = jax.ShapeDtypeStruct((pairs, 2, HALF, PAIR), BF16)
    half_wide = jax.ShapeDtypeStruct((pairs, 2, HALF, PAIR), F32)

    query, key, value, grad, cosine, sine, theirs, mine = call(
        states_kernel,
        [like] * 4 + [table] * 2 + [half_low, half_wide],
        positions.reshape(1, tokens), query_rows, key_rows, value_rows, out_grad,
        in_specs=[VMEM] + [HBM] * 4,
        out_specs=[VMEM] * 8,
        scratch=[pltpu.VMEM((tokens, width), BF16)] * 2 + [pltpu.SemaphoreType.DMA((groups, 4))],
    )
    theirs = lax.all_gather(theirs, "core")
    chip = call(chip_kernel, half_low, mine, theirs)
    over_z = lax.all_to_all(chip, "z", 0, 0, tiled=True)

    query_in, key_in, value_in = call(
        block_kernel, [wide] * 3, query, key, value, grad, out_specs=[VMEM] * 3, flops=24 * SPAN**3 * pairs
    )

    group = call(totals_kernel, jax.ShapeDtypeStruct((n_ctx, HALF, PAIR), F32), over_z)
    over_ctx = lax.all_to_all(group, "ctx", 0, 0, tiled=True)
    sums = call(scan_kernel, half_low, over_z, over_ctx)
    back = lax.all_to_all(sums, "z", 0, 0, tiled=True)
    sent = lax.all_gather(call(send_kernel, half_low, back, mine), "core")

    return call(
        functools.partial(finish_kernel, factor),
        [like] * 3,
        key, value, grad, cosine, sine, back, theirs, sent, query_in, key_in, value_in,
        out_specs=[HBM] * 3,
        scratch=[pltpu.VMEM((tokens, width), BF16)] * 3 + [pltpu.SemaphoreType.DMA((groups, 3))],
    )


def solution(mesh):
    split = Mesh(
        mesh.devices.reshape(mesh.shape["ctx"], mesh.shape["sp"] // 2, 2), ("ctx", "z", "core")
    )
    tokens = ("ctx", "z", "core")
    return jax.shard_map(
        on_device,
        mesh=split,
        in_specs=(P(tokens, None),) * 4 + (P(tokens),),
        out_specs=(P(tokens, None),) * 3,
        check_vma=False,
    )
```

time: 95.2 us -> 88.4 us (0.929)
  blocking collectives: 58.9 us -> 55 us
  waiting for transfers between devices: 5.77 us -> 4.51 us
    all_to_all x2 -> x0, blocking collectives: 21.5 us -> none  [the longest x1 10.8 us: on_device(): carried = lax.all_to_all(spread, 'core', 0, 0, tiled=True)]
    all_gather x0 -> x2, blocking collectives: none -> 17.5 us  [the longest x1 8.84 us: on_device(): sent = lax.all_gather(call(send_kernel, half_low, back, mine), 'core')]
    all_to_all x1, waiting for transfers between devices: 5.77 us -> 4.51 us  [on_device(): back = lax.all_to_all(sums, 'z', 0, 0, tiled=True)]
where the time goes in v1:
time: 88.4 us; the launch traced here: 87.8 us
  blocking collectives  55 us (62%)
  starting transfers between devices  10.2 us (12%)
  Pallas kernels  9.42 us (11%)
  local copies, waits for them, and re-layouts  7.9 us (9%)
  waiting for transfers between devices  4.51 us (5%)
    all_to_all x1, blocking collectives, on_device(): over_z = lax.all_to_all(chip, 'z', 0, 0, tiled=True)  23.4 us
    all_to_all x1, blocking collectives, on_device(): over_ctx = lax.all_to_all(group, 'ctx', 0, 0, tiled=True)  14.1 us
    all_to_all x1, starting transfers between devices, on_device(): back = lax.all_to_all(sums, 'z', 0, 0, tiled=True)  10.2 us
    pallas_call x7, Pallas kernels, call(): pl.pallas_call(kernel, out_shape=placed, in_specs=in_specs, out_specs=out...  9.42 us
    all_gather x1, blocking collectives, on_device(): sent = lax.all_gather(call(send_kernel, half_low, back, mine), 'core')  8.84 us
    all_gather x1, blocking collectives, on_device(): theirs = lax.all_gather(theirs, 'core')  8.69 us
    unnamed x28, local copies, waits for them, and re-layouts  7.9 us
    all_to_all x1, waiting for transfers between devices, on_device(): back = lax.all_to_all(sums, 'z', 0, 0, tiled=True)  4.51 us
  transfers between devices with their start and end apart: 1, of which 1 were waited for; matrix products, arithmetic and copies ran while one was open for 0% of the time, Pallas kernels for 4%

profile of v1, /device:TPU:1, one launch (start us, length us, event | category | flops | bytes accessed | tf_op | source)
XLA Modules:
  0.0 87.8 jit_solution(16322067443836738088)
XLA Ops:
  0.6 0.0 copy-start.11
  0.6 0.6 copy-done.11
  1.3 3.1 %shard_map.76 = (bf16[128,2048]{1,0:T(8,128)(2,1)S(1)}, bf16[128,2048]{1,0:T(8,128)(2,1)S(1)}, bf16[128,2048]{1,0:T(8,128)(2,1)S(1)}, bf16[128,2048]{1,0:T(8,128...) custom-call(s32[1,128]{1,0:T(1,128)S(1)} %bitcast.6, ...), custom_call_target="tpu_custom_call" | custom-call | bytes 1048576 | tf_op jit(solution)/shard_map/pallas_call | solution.py:216
  4.4 0.0 copy-start.2
  4.4 0.0 copy-start.5
  4.4 0.0 copy-start.8
  4.4 0.0 copy-start.12
  4.4 8.7 %all-gather = bf16[32,2,32,128]{3,2,1,0:T(8,128)(2,1)S(1)} all-gather(bf16[16,2,32,128]{3,2,1,0:T(8,128)(2,1)S(1)} %get-tuple-element.20), channel_id=2, replica_groups=mesh['ctx'=16,'z'=16,'core'=2] {'core'}, dimensions={0}, use_global_device_ids=true | all-gather | bytes 786432 | tf_op jit(solution)/shard_map/all_gather | solution.py:248
  13.1 0.0 copy-done.2
  13.2 0.0 copy-done.5
  13.2 0.0 copy-done.8
  13.2 0.0 copy-done.12
  13.2 23.4 %all_to_all.15.zr_ref = bf16[16,2,32,128]{3,2,1,0:T(8,128)(2,1)S(1)} all-to-all(bf16[16,2,32,128]{3,2,1,0:T(8,128)(2,1)S(1)} %shard_map.77), channel_id=1, replica_groups=mesh['ctx'=16,'z'=16,'core'=2] {'z'}, dimensions={0} | all-to-all | bytes 524288 | tf_op jit(solution)/shard_map/all_to_all | solution.py:250
  36.5 0.1 shard_map.78
  36.6 14.1 %all_to_all.16.cx_ref = f32[16,32,128]{2,1,0:T(8,128)S(1)} all-to-all(f32[16,32,128]{2,1,0:T(8,128)S(1)} %shard_map.78), channel_id=1, replica_groups=mesh['ctx'=16,'z'=16,'core'=2] {'ctx'}, dimensions={0} | all-to-all | bytes 524288 | tf_op jit(solution)/shard_map/all_to_all | solution.py:257
  50.7 0.8 shard_map.79
  51.5 10.2 %all-to-all-start.2 = ((bf16[16,2,32,128]{3,2,1,0:T(8,128)(2,1)}), bf16[16,2,32,128]{3,2,1,0:T(8,128)(2,1)S(1)}, u32[]{:S(2)}, u32[]{:S(2)}) async-start(bf16[16,2,32,128]{3,2,1,0:T(8,128)(2,1)} %shard_map.79), calls=%async_computation.2 | async-start | bytes 524288 | tf_op jit(solution)/shard_map/all_to_all | solution.py:259
  61.7 0.0 copy-start.3
  61.7 1.0 %copy-done.3 = bf16[128,2048]{1,0:T(8,128)(2,1)S(1)} copy-done((bf16[128,2048]{1,0:T(8,128)(2,1)S(1)}, bf16[128,2048]{1,0:T(8,128)(2,1)}, u32[]{:S(2)}) %copy-start.3) | copy-done | bytes 524312
  62.8 1.0 %copy-done.6 = bf16[128,2048]{1,0:T(8,128)(2,1)S(1)} copy-done((bf16[128,2048]{1,0:T(8,128)(2,1)S(1)}, bf16[128,2048]{1,0:T(8,128)(2,1)}, u32[]{:S(2)}) %copy-start.6) | copy-done | bytes 524312
  63.8 1.0 %copy-done.9 = bf16[128,2048]{1,0:T(8,128)(2,1)S(1)} copy-done((bf16[128,2048]{1,0:T(8,128)(2,1)S(1)}, bf16[128,2048]{1,0:T(8,128)(2,1)}, u32[]{:S(2)}) %copy-start.9) | copy-done | bytes 524312
  64.9 1.0 %copy-done.13 = bf16[128,2048]{1,0:T(8,128)(2,1)S(1)} copy-done((bf16[128,2048]{1,0:T(8,128)(2,1)S(1)}, bf16[128,2048]{1,0:T(8,128)(2,1)}, u32[]{:S(2)}) %copy-start.13) | copy-done | bytes 524312
  65.9 3.1 %shard_map.81 = (f32[128,2048]{1,0:T(8,128)S(1)}, f32[128,2048]{1,0:T(8,128)S(1)}, f32[128,2048]{1,0:T(8,128)S(1)}) custom-call(bf16[128,2048]{1,0:T(8,128)(2,1)S(1)} %copy-done.13, bf16[128,2048]{1,0:T(8,128)(2,1)S(1)} %copy-done.3, bf16[128,2048]{1,0:T(8,128)(2,1)S(1)} %copy-done.6, bf16[128,2048]{1,0:T(8,128)(2,1)S(1)} %copy-done.9), custom_call_target="tpu_custom_call" | custom-call | flops 805306368 | bytes 1048576 | tf_op jit(solution)/shard_map/pallas_call | solution.py:216
  69.0 0.0 copy-start
  69.0 1.0 %copy-done = f32[128,2048]{1,0:T(8,128)} copy-done((f32[128,2048]{1,0:T(8,128)}, f32[128,2048]{1,0:T(8,128)S(1)}, u32[]{:S(2)}) %copy-start) | copy-done | bytes 1048600
  70.0 4.5 %all-to-all-done.2.zb_ref = bf16[16,2,32,128]{3,2,1,0:T(8,128)(2,1)S(1)} async-done(((bf16[16,2,32,128]{3,2,1,0:T(8,128)(2,1)}), bf16[16,2,32,128]{3,2,1,0:T(8,128)(2,1)S(1)}, u32[]{:S(2)}, u32[]{:S(2)}) %all-to-all-start.2) | async-done | bytes 262176 | tf_op jit(solution)/shard_map/all_to_all | solution.py:259
  74.5 0.1 shard_map.80
  74.6 0.0 copy-start.4
  74.6 8.8 %all-gather.1 = bf16[32,2,32,128]{3,2,1,0:T(8,128)(2,1)S(1)} all-gather(bf16[16,2,32,128]{3,2,1,0:T(8,128)(2,1)S(1)} %shard_map.80), channel_id=3, replica_groups=mesh['ctx'=16,'z'=16,'core'=2] {'core'}, dimensions={0}, use_global_device_ids=true | all-gather | bytes 786432 | tf_op jit(solution)/shard_map/all_gather | solution.py:260
  83.4 1.0 %copy-done.7 = bf16[128,2048]{1,0:T(8,128)(2,1)S(1)} copy-done((bf16[128,2048]{1,0:T(8,128)(2,1)S(1)}, bf16[128,2048]{1,0:T(8,128)(2,1)}, u32[]{:S(2)}) %copy-start.7) | copy-done | bytes 524312
  84.5 1.0 %copy-done.10 = bf16[128,2048]{1,0:T(8,128)(2,1)S(1)} copy-done((bf16[128,2048]{1,0:T(8,128)(2,1)S(1)}, bf16[128,2048]{1,0:T(8,128)(2,1)}, u32[]{:S(2)}) %copy-start.10) | copy-done | bytes 524312
  85.5 2.3 %shard_map.82 = (bf16[128,2048]{1,0:T(8,128)(2,1)}, bf16[128,2048]{1,0:T(8,128)(2,1)}, bf16[128,2048]{1,0:T(8,128)(2,1)}) custom-call(bf16[128,2048]{1,0:T(8,128)(2,1)S(1)} %copy-done.4, bf16[128,2048]{1,0:T(8,128)(2,1)S(1)} %copy-done.7, bf16[128,2048]{1,0:T(8,128)(2,1)S(1)} %copy-done.10, f32[128,128]{1,0:T(8,128)S(1)} %get-tuple-element.17.cos_ref, ...), custom_call_target="tpu_custom_call" | custom-call | bytes 1048576 | tf_op jit(solution)/shard_map/pallas_call | solution.py:216
  (9 shorter events, 0.1 us)
Async XLA Ops:
  0.6 0.7 copy-start.11
  4.4 8.7 %copy-start.2 = (bf16[128,2048]{1,0:T(8,128)(2,1)}, bf16[128,2048]{1,0:T(8,128)(2,1)S(1)}, u32[]{:S(2)}) copy-start(bf16[128,2048]{1,0:T(8,128)(2,1)S(1)} %get-tuple-element.14.k_ref) | copy-start | bytes 1572868
  4.4 8.8 %copy-start.5 = (bf16[128,2048]{1,0:T(8,128)(2,1)}, bf16[128,2048]{1,0:T(8,128)(2,1)S(1)}, u32[]{:S(2)}) copy-start(bf16[128,2048]{1,0:T(8,128)(2,1)S(1)} %get-tuple-element.15.v_ref) | copy-start | bytes 1572868
  4.4 8.8 %copy-start.8 = (bf16[128,2048]{1,0:T(8,128)(2,1)}, bf16[128,2048]{1,0:T(8,128)(2,1)S(1)}, u32[]{:S(2)}) copy-start(bf16[128,2048]{1,0:T(8,128)(2,1)S(1)} %get-tuple-element.16.g_ref) | copy-start | bytes 1572868
  4.4 8.8 %copy-start.12 = (bf16[128,2048]{1,0:T(8,128)(2,1)}, bf16[128,2048]{1,0:T(8,128)(2,1)S(1)}, u32[]{:S(2)}) copy-start(bf16[128,2048]{1,0:T(8,128)(2,1)S(1)} %get-tuple-element.21.q_ref) | copy-start | bytes 1572868
  51.5 23.0 %all-to-all-start.2 = ((bf16[16,2,32,128]{3,2,1,0:T(8,128)(2,1)}), bf16[16,2,32,128]{3,2,1,0:T(8,128)(2,1)S(1)}, u32[]{:S(2)}, u32[]{:S(2)}) async-start(bf16[16,2,32,128]{3,2,1,0:T(8,128)(2,1)} %shard_map.79), calls=%async_computation.2 | async-start | bytes 524288 | tf_op jit(solution)/shard_map/all_to_all | solution.py:259
  61.7 1.0 %copy-start.3 = (bf16[128,2048]{1,0:T(8,128)(2,1)S(1)}, bf16[128,2048]{1,0:T(8,128)(2,1)}, u32[]{:S(2)}) copy-start(bf16[128,2048]{1,0:T(8,128)(2,1)} %copy-done.2) | copy-start | bytes 1572868
  62.8 1.0 %copy-start.6 = (bf16[128,2048]{1,0:T(8,128)(2,1)S(1)}, bf16[128,2048]{1,0:T(8,128)(2,1)}, u32[]{:S(2)}) copy-start(bf16[128,2048]{1,0:T(8,128)(2,1)} %copy-done.5) | copy-start | bytes 1572868
  63.8 1.0 %copy-start.9 = (bf16[128,2048]{1,0:T(8,128)(2,1)S(1)}, bf16[128,2048]{1,0:T(8,128)(2,1)}, u32[]{:S(2)}) copy-start(bf16[128,2048]{1,0:T(8,128)(2,1)} %copy-done.8) | copy-start | bytes 1572868
  64.9 1.0 %copy-start.13 = (bf16[128,2048]{1,0:T(8,128)(2,1)S(1)}, bf16[128,2048]{1,0:T(8,128)(2,1)}, u32[]{:S(2)}) copy-start(bf16[128,2048]{1,0:T(8,128)(2,1)} %copy-done.12) | copy-start | bytes 1572868
  69.0 1.0 %copy-start = (f32[128,2048]{1,0:T(8,128)}, f32[128,2048]{1,0:T(8,128)S(1)}, u32[]{:S(2)}) copy-start(f32[128,2048]{1,0:T(8,128)S(1)} %get-tuple-element.24.vi_ref) | copy-start | bytes 3145732
  74.5 8.9 %copy-start.1 = (f32[128,2048]{1,0:T(8,128)S(1)}, f32[128,2048]{1,0:T(8,128)}, u32[]{:S(2)}) copy-start(f32[128,2048]{1,0:T(8,128)} %copy-done) | copy-start | bytes 3145732
  74.6 8.9 %copy-start.4 = (bf16[128,2048]{1,0:T(8,128)(2,1)S(1)}, bf16[128,2048]{1,0:T(8,128)(2,1)}, u32[]{:S(2)}) copy-start(bf16[128,2048]{1,0:T(8,128)(2,1)} %copy-done.2) | copy-start | bytes 1572868
  83.4 1.0 %copy-start.7 = (bf16[128,2048]{1,0:T(8,128)(2,1)S(1)}, bf16[128,2048]{1,0:T(8,128)(2,1)}, u32[]{:S(2)}) copy-start(bf16[128,2048]{1,0:T(8,128)(2,1)} %copy-done.5) | copy-start | bytes 1572868
  84.5 1.0 %copy-start.10 = (bf16[128,2048]{1,0:T(8,128)(2,1)S(1)}, bf16[128,2048]{1,0:T(8,128)(2,1)}, u32[]{:S(2)}) copy-start(bf16[128,2048]{1,0:T(8,128)(2,1)} %copy-done.8) | copy-start | bytes 1572868

commit v2 on v1

--- a/solution.py
+++ b/solution.py
@@ -68,38 +68,57 @@
     return pl.ds(pl.multiple_of(first * PAIR, PAIR), count * PAIR)
 
 
+def loads(sources, sems, first):
+    pairs = sources[0][0].shape[1] // PAIR
+    groups = []
+    for group in range(pairs // GROUP):
+        at = span(lax.rem(first + group * GROUP, pairs), GROUP)
+        groups.append(
+            [
+                pltpu.make_async_copy(src.at[:, at], dst.at[:, at], sems.at[group, i])
+                for i, (src, dst) in enumerate(sources)
+            ]
+        )
+    for copies in groups:
+        for copy in copies:
+            copy.start()
+    return groups
+
+
+def store(results, sems, first, group):
+    pairs = results[0][0].shape[1] // PAIR
+    at = span(lax.rem(first + group * GROUP, pairs), GROUP)
+    copies = [
+        pltpu.make_async_copy(src.at[:, at], dst.at[:, at], sems.at[group, i])
+        for i, (src, dst) in enumerate(results)
+    ]
+    for copy in copies:
+        copy.start()
+    return copies
+
+
 def states_kernel(
-    pos_ref, q_in, k_in, v_in, g_in,
-    qr_ref, kr_ref, v_ref, g_ref, cos_ref, sin_ref, theirs_ref, mine_ref,
-    q_ref, k_ref, sems,
+    pos_in, q_in, k_in, v_in, g_in,
+    cos_ref, sin_ref, theirs_ref, mine_ref,
+    pos_ref, q_ref, k_ref, v_ref, g_ref, sems, pos_sem,
 ):
     pairs = q_ref.shape[1] // PAIR
     core = lax.axis_index("core")
     first = (1 - core) * (pairs // 2)
-    sources = ((q_in, q_ref), (k_in, k_ref), (v_in, v_ref), (g_in, g_ref))
-
-    def copies(group):
-        at = span(lax.rem(first + group * GROUP, pairs), GROUP)
-        return [
-            pltpu.make_async_copy(src.at[:, at], dst.at[:, at], sems.at[group, i])
-            for i, (src, dst) in enumerate(sources)
-        ]
-
-    for group in range(pairs // GROUP):
-        for copy in copies(group):
-            copy.start()
+    pos_copy = pltpu.make_async_copy(pos_in, pos_ref, pos_sem)
+    pos_copy.start()
+    groups = loads(((q_in, q_ref), (k_in, k_ref), (v_in, v_ref), (g_in, g_ref)), sems, first)
+    pos_copy.wait()
     cosine, sine = angle_tables(pos_ref[...])
     cos_ref[...] = cosine
     sin_ref[...] = sine
     for j in range(pairs):
         if j % GROUP == 0:
-            for copy in copies(j // GROUP):
+            for copy in groups[j // GROUP]:
                 copy.wait()
         at = span(lax.rem(first + j, pairs))
         q = rotated(q_ref[:, at], cosine, sine).astype(BF16)
         k = rotated(k_ref[:, at], cosine, sine).astype(BF16)
-        qr_ref[:, at] = q
-        kr_ref[:, at] = k
         state = pack_pair(dot(k, v_ref[:, at], TN))
         grad = pack_pair(dot(q, g_ref[:, at], TN))
         out, slot = (theirs_ref, 2 * j) if j < pairs // 2 else (mine_ref, 2 * j - pairs)
@@ -109,14 +128,27 @@
             out[slot + r, 1] = grad[rows].astype(out.dtype)
 
 
-def block_kernel(q_ref, k_ref, v_ref, g_ref, qo_ref, ko_ref, vo_ref):
+def block_kernel(
+    q_in, k_in, v_in, g_in, cos_ref, sin_ref, kr_out, q_out, k_out, v_out,
+    q_ref, k_ref, v_ref, g_ref, kr_ref, qo_ref, ko_ref, vo_ref, sems, out_sems,
+):
+    groups = loads(((q_in, q_ref), (k_in, k_ref), (v_in, v_ref), (g_in, g_ref)), sems, 0)
+    results = ((kr_ref, kr_out), (qo_ref, q_out), (ko_ref, k_out), (vo_ref, v_out))
+    cosine, sine = cos_ref[...], sin_ref[...]
     row = lax.broadcasted_iota(jnp.int32, (SPAN, 2 * SPAN), 0)
     col = lax.broadcasted_iota(jnp.int32, (SPAN, 2 * SPAN), 1) % SPAN
     lower = row >= col
     upper = row <= col
+    stores = []
     for p in range(q_ref.shape[1] // PAIR):
+        if p % GROUP == 0:
+            for copy in groups[p // GROUP]:
+                copy.wait()
         at = slice(p * PAIR, (p + 1) * PAIR)
-        q, k, v, g = q_ref[:, at], k_ref[:, at], v_ref[:, at], g_ref[:, at]
+        q = rotated(q_ref[:, at], cosine, sine).astype(BF16)
+        k = rotated(k_ref[:, at], cosine, sine).astype(BF16)
+        v, g = v_ref[:, at], g_ref[:, at]
+        kr_ref[:, at] = k
         q2, k2, v2, g2 = by_head(q), by_head(k), by_head(v), by_head(g)
         w = jnp.where(lower, dot(g, v2, NT), 0.0).astype(BF16)
         wt = jnp.where(upper, dot(v, g2, NT), 0.0).astype(BF16)
@@ -124,6 +156,10 @@
         qo_ref[:, at] = dot(w, k2, NN)
         ko_ref[:, at] = dot(wt, q2, NN)
         vo_ref[:, at] = dot(st, g2, NN)
+        if p % GROUP == GROUP - 1:
+            stores += store(results, out_sems, 0, p // GROUP)
+    for copy in stores:
+        copy.wait()
 
 
 def chip_kernel(mine_ref, theirs_ref, out_ref):
@@ -132,7 +168,8 @@
         out_ref[z] = (mine_ref[z] + theirs_ref[other, z].astype(F32)).astype(BF16)
 
 
-def totals_kernel(zr_ref, out_ref):
+def totals_kernel(zr_ref, ready_in, out_ref):
+    del ready_in
     state = zr_ref[0, 0].astype(F32)
     grad = zr_ref[0, 1].astype(F32)
     for z in range(1, zr_ref.shape[0]):
@@ -167,16 +204,16 @@
 
 
 def finish_kernel(
-    factor, k_ref, v_ref, g_ref, cos_ref, sin_ref, zb_ref, theirs_ref, sent_ref, qi_ref, ki_ref, vi_ref,
-    q_out, k_out, v_out, qo_ref, ko_ref, vo_ref, sems,
+    factor, k_ref, v_ref, g_ref, qi_ref, ki_ref, vi_ref, cos_ref, sin_ref, zb_ref, theirs_ref, sent_ref,
+    q_out, k_out, v_out, qo_ref, ko_ref, vo_ref, out_sems,
 ):
     pairs = k_ref.shape[1] // PAIR
     core = lax.axis_index("core")
     other = 1 - core
     first = core * (pairs // 2)
+    results = ((qo_ref, q_out), (ko_ref, k_out), (vo_ref, v_out))
     cosine, sine = cos_ref[...], -sin_ref[...]
-    results = ((qo_ref, q_out), (ko_ref, k_out), (vo_ref, v_out))
-    copies = []
+    stores = []
 
     def carried(slot, kind):
         count = zb_ref.shape[0]
@@ -196,12 +233,8 @@
         qo_ref[:, at] = rotated(qo, cosine, sine).astype(BF16)
         ko_ref[:, at] = rotated(ko, cosine, sine).astype(BF16)
         if j % GROUP == GROUP - 1:
-            group = j // GROUP
-            done = span(lax.rem(first + group * GROUP, pairs), GROUP)
-            for i, (src, dst) in enumerate(results):
-                copies.append(pltpu.make_async_copy(src.at[:, done], dst.at[:, done], sems.at[group, i]))
-                copies[-1].start()
-    for copy in copies:
+            stores += store(results, out_sems, first, j // GROUP)
+    for copy in stores:
         copy.wait()
 
 
@@ -237,23 +270,36 @@
     half_low = jax.ShapeDtypeStruct((pairs, 2, HALF, PAIR), BF16)
     half_wide = jax.ShapeDtypeStruct((pairs, 2, HALF, PAIR), F32)
 
-    query, key, value, grad, cosine, sine, theirs, mine = call(
+    low, high = pltpu.VMEM((tokens, width), BF16), pltpu.VMEM((tokens, width), F32)
+
+    def sems(count):
+        return pltpu.SemaphoreType.DMA((groups, count))
+
+    cosine, sine, theirs, mine = call(
         states_kernel,
-        [like] * 4 + [table] * 2 + [half_low, half_wide],
+        [table] * 2 + [half_low, half_wide],
         positions.reshape(1, tokens), query_rows, key_rows, value_rows, out_grad,
-        in_specs=[VMEM] + [HBM] * 4,
-        out_specs=[VMEM] * 8,
-        scratch=[pltpu.VMEM((tokens, width), BF16)] * 2 + [pltpu.SemaphoreType.DMA((groups, 4))],
+        in_specs=[HBM] * 5,
+        out_specs=[VMEM] * 4,
+        scratch=[pltpu.VMEM((1, tokens), jnp.int32)] + [low] * 4 + [sems(4), pltpu.SemaphoreType.DMA],
     )
     theirs = lax.all_gather(theirs, "core")
     chip = call(chip_kernel, half_low, mine, theirs)
     over_z = lax.all_to_all(chip, "z", 0, 0, tiled=True)
 
-    query_in, key_in, value_in = call(
-        block_kernel, [wide] * 3, query, key, value, grad, out_specs=[VMEM] * 3, flops=24 * SPAN**3 * pairs
-    )
-
-    group = call(totals_kernel, jax.ShapeDtypeStruct((n_ctx, HALF, PAIR), F32), over_z)
+    key, query_in, key_in, value_in = call(
+        block_kernel,
+        [like] + [wide] * 3,
+        query_rows, key_rows, value_rows, out_grad, cosine, sine,
+        in_specs=[HBM] * 4 + [VMEM] * 2,
+        out_specs=[HBM] * 4,
+        scratch=[low] * 5 + [high] * 3 + [sems(4), sems(4)],
+        flops=24 * SPAN**3 * pairs,
+    )
+
+    group = call(
+        totals_kernel, jax.ShapeDtypeStruct((n_ctx, HALF, PAIR), F32), over_z, query_in, in_specs=[VMEM, HBM]
+    )
     over_ctx = lax.all_to_all(group, "ctx", 0, 0, tiled=True)
     sums = call(scan_kernel, half_low, over_z, over_ctx)
     back = lax.all_to_all(sums, "z", 0, 0, tiled=True)
@@ -262,9 +308,9 @@
     return call(
         functools.partial(finish_kernel, factor),
         [like] * 3,
-        key, value, grad, cosine, sine, back, theirs, sent, query_in, key_in, value_in,
+        key, value_rows, out_grad, query_in, key_in, value_in, cosine, sine, back, theirs, sent,
         out_specs=[HBM] * 3,
-        scratch=[pltpu.VMEM((tokens, width), BF16)] * 3 + [pltpu.SemaphoreType.DMA((groups, 3))],
+        scratch=[low] * 3 + [sems(3)],
     )
 
 

time: 88.4 us -> 85.6 us (0.968)
  local copies, waits for them, and re-layouts: 7.9 us -> 0.03 us
  waiting for transfers between devices: 4.51 us -> 8.13 us
  Pallas kernels: 9.42 us -> 12.2 us
    unnamed x28 -> x12, local copies, waits for them, and re-layouts: 7.9 us -> 0.03 us
    all_to_all x1, waiting for transfers between devices: 4.51 us -> 8.13 us  [on_device(): over_z = lax.all_to_all(chip, 'z', 0, 0, tiled=True)]
    pallas_call x7, Pallas kernels: 9.42 us -> 12.2 us  [call(): pl.pallas_call(kernel, out_shape=placed, in_specs=in_specs, out_specs=out...]
  transfers between devices with their start and end apart: 1 -> 1, of which waited for: 1 -> 1; matrix products, arithmetic and copies ran while one was open for 0% -> 0% of each run, Pallas kernels for 4% -> 7%
where the time goes in v2:
time: 85.6 us; the launch traced here: 85.3 us
  blocking collectives  54.7 us (64%)
  Pallas kernels  12.2 us (14%)
  starting transfers between devices  9.54 us (11%)
  waiting for transfers between devices  8.13 us (9%)
    all_to_all x1, blocking collectives, on_device(): back = lax.all_to_all(sums, 'z', 0, 0, tiled=True)  22.9 us
    all_to_all x1, blocking collectives, on_device(): over_ctx = lax.all_to_all(group, 'ctx', 0, 0, tiled=True)  14.2 us
    pallas_call x7, Pallas kernels, call(): pl.pallas_call(kernel, out_shape=placed, in_specs=in_specs, out_specs=out...  12.2 us
    all_to_all x1, starting transfers between devices, on_device(): over_z = lax.all_to_all(chip, 'z', 0, 0, tiled=True)  9.54 us
    all_gather x1, blocking collectives, on_device(): sent = lax.all_gather(call(send_kernel, half_low, back, mine), 'core')  8.84 us
    all_gather x1, blocking collectives, on_device(): theirs = lax.all_gather(theirs, 'core')  8.69 us
    all_to_all x1, waiting for transfers between devices, on_device(): over_z = lax.all_to_all(chip, 'z', 0, 0, tiled=True)  8.13 us
  transfers between devices with their start and end apart: 1, of which 1 were waited for; matrix products, arithmetic and copies ran while one was open for 0% of the time, Pallas kernels for 7%

profile of v2, /device:TPU:1, one launch (start us, length us, event | category | flops | bytes accessed | tf_op | source)
XLA Modules:
  0.0 85.3 jit_solution(13690173872317073367)
XLA Ops:
  0.6 3.0 %shard_map.76 = (f32[128,128]{1,0:T(8,128)S(1)}, f32[128,128]{1,0:T(8,128)S(1)}, bf16[16,2,32,128]{3,2,1,0:T(8,128)(2,1)S(1)}, f32[16,2,32,128]{3,2,1,0:T(8,128)S(1)}) custom-call(s32[1,128]{1,0:T(1,128)} %bitcast.6, bf16[128,2048]{1,0:T(8,128)(2,1)} %q_in.3, bf16[128,2048]{1,0:T(8,128)(2,1)} %k_in.3, bf16[128,2048]{1,0:T(8,128)(2,1)} %v_ref.1, ...), custom_call_target="tpu_custom_call" | custom-call | bytes 1048576 | tf_op jit(solution)/shard_map/pallas_call | solution.py:249
  3.7 8.7 %all-gather = bf16[32,2,32,128]{3,2,1,0:T(8,128)(2,1)S(1)} all-gather(bf16[16,2,32,128]{3,2,1,0:T(8,128)(2,1)S(1)} %get-tuple-element.18), channel_id=2, replica_groups=mesh['ctx'=16,'z'=16,'core'=2] {'core'}, dimensions={0}, use_global_device_ids=true | all-gather | bytes 786432 | tf_op jit(solution)/shard_map/all_gather | solution.py:286
  12.4 0.7 shard_map.78
  13.1 9.5 %all-to-all-start = ((bf16[16,2,32,128]{3,2,1,0:T(8,128)(2,1)}), bf16[16,2,32,128]{3,2,1,0:T(8,128)(2,1)S(1)}, u32[]{:S(2)}, u32[]{:S(2)}) async-start(bf16[16,2,32,128]{3,2,1,0:T(8,128)(2,1)} %shard_map.78), calls=%async_computation | async-start | bytes 524288 | tf_op jit(solution)/shard_map/all_to_all | solution.py:288
  22.7 5.9 %shard_map.77 = (bf16[128,2048]{1,0:T(8,128)(2,1)}, f32[128,2048]{1,0:T(8,128)}, f32[128,2048]{1,0:T(8,128)}, f32[128,2048]{1,0:T(8,128)}) custom-call(bf16[128,2048]{1,0:T(8,128)(2,1)} %q_in.3, bf16[128,2048]{1,0:T(8,128)(2,1)} %k_in.3, bf16[128,2048]{1,0:T(8,128)(2,1)} %v_ref.1, bf16[128,2048]{1,0:T(8,128)(2,1)} %g_ref.1, ...), custom_call_target="tpu_custom_call" | custom-call | flops 805306368 | bytes 1048576 | tf_op jit(solution)/shard_map/pallas_call | solution.py:249
  28.5 8.1 %all-to-all-done.zr_ref = bf16[16,2,32,128]{3,2,1,0:T(8,128)(2,1)S(1)} async-done(((bf16[16,2,32,128]{3,2,1,0:T(8,128)(2,1)}), bf16[16,2,32,128]{3,2,1,0:T(8,128)(2,1)S(1)}, u32[]{:S(2)}, u32[]{:S(2)}) %all-to-all-start) | async-done | bytes 262176 | tf_op jit(solution)/shard_map/all_to_all | solution.py:288
  36.7 0.0 copy-start.4
  36.7 0.1 shard_map.79
  36.7 0.0 copy-start.5
  36.7 14.2 %all_to_all.15.cx_ref = f32[16,32,128]{2,1,0:T(8,128)S(1)} all-to-all(f32[16,32,128]{2,1,0:T(8,128)S(1)} %shard_map.79), channel_id=1, replica_groups=mesh['ctx'=16,'z'=16,'core'=2] {'ctx'}, dimensions={0} | all-to-all | bytes 524288 | tf_op jit(solution)/shard_map/all_to_all | solution.py:303
  51.0 0.0 copy-start.3
  51.0 0.1 shard_map.80
  51.1 0.0 copy-start.2
  51.1 22.9 %all_to_all.16.zb_ref = bf16[16,2,32,128]{3,2,1,0:T(8,128)(2,1)S(1)} all-to-all(bf16[16,2,32,128]{3,2,1,0:T(8,128)(2,1)S(1)} %shard_map.80), channel_id=1, replica_groups=mesh['ctx'=16,'z'=16,'core'=2] {'z'}, dimensions={0} | all-to-all | bytes 524288 | tf_op jit(solution)/shard_map/all_to_all | solution.py:305
  74.0 0.0 copy-start
  74.0 0.1 shard_map.81
  74.1 0.0 copy-start.1
  74.1 8.8 %all-gather.1 = bf16[32,2,32,128]{3,2,1,0:T(8,128)(2,1)S(1)} all-gather(bf16[16,2,32,128]{3,2,1,0:T(8,128)(2,1)S(1)} %shard_map.81), channel_id=3, replica_groups=mesh['ctx'=16,'z'=16,'core'=2] {'core'}, dimensions={0}, use_global_device_ids=true | all-gather | bytes 786432 | tf_op jit(solution)/shard_map/all_gather | solution.py:306
  82.9 0.0 copy-done.4
  82.9 0.0 copy-done.5
  82.9 0.0 copy-done.3
  82.9 0.0 copy-done.2
  83.0 0.0 copy-done
  83.0 0.0 copy-done.1
  83.0 2.3 %shard_map.82 = (bf16[128,2048]{1,0:T(8,128)(2,1)}, bf16[128,2048]{1,0:T(8,128)(2,1)}, bf16[128,2048]{1,0:T(8,128)(2,1)}) custom-call(bf16[128,2048]{1,0:T(8,128)(2,1)S(1)} %copy-done.5, bf16[128,2048]{1,0:T(8,128)(2,1)S(1)} %copy-done.1, bf16[128,2048]{1,0:T(8,128)(2,1)S(1)} %copy-done.2, f32[128,2048]{1,0:T(8,128)S(1)} %copy-done, ...), custom_call_target="tpu_custom_call" | custom-call | bytes 1048576 | tf_op jit(solution)/shard_map/pallas_call | solution.py:249
Async XLA Ops:
  13.1 23.6 %all-to-all-start = ((bf16[16,2,32,128]{3,2,1,0:T(8,128)(2,1)}), bf16[16,2,32,128]{3,2,1,0:T(8,128)(2,1)S(1)}, u32[]{:S(2)}, u32[]{:S(2)}) async-start(bf16[16,2,32,128]{3,2,1,0:T(8,128)(2,1)} %shard_map.78), calls=%async_computation | async-start | bytes 524288 | tf_op jit(solution)/shard_map/all_to_all | solution.py:288
  36.7 46.3 %copy-start.4 = (f32[128,2048]{1,0:T(8,128)S(1)}, f32[128,2048]{1,0:T(8,128)}, u32[]{:S(2)}) copy-start(f32[128,2048]{1,0:T(8,128)} %get-tuple-element.16.vi_ref) | copy-start | bytes 3145732
  36.7 46.2 %copy-start.5 = (bf16[128,2048]{1,0:T(8,128)(2,1)S(1)}, bf16[128,2048]{1,0:T(8,128)(2,1)}, u32[]{:S(2)}) copy-start(bf16[128,2048]{1,0:T(8,128)(2,1)} %get-tuple-element.13.k_ref) | copy-start | bytes 1572868
  51.0 32.0 %copy-start.3 = (f32[128,2048]{1,0:T(8,128)S(1)}, f32[128,2048]{1,0:T(8,128)}, u32[]{:S(2)}) copy-start(f32[128,2048]{1,0:T(8,128)} %get-tuple-element.15.ki_ref) | copy-start | bytes 3145732
  51.1 31.9 %copy-start.2 = (bf16[128,2048]{1,0:T(8,128)(2,1)S(1)}, bf16[128,2048]{1,0:T(8,128)(2,1)}, u32[]{:S(2)}) copy-start(bf16[128,2048]{1,0:T(8,128)(2,1)} %g_ref.1) | copy-start | bytes 1572868
  74.0 8.9 %copy-start = (f32[128,2048]{1,0:T(8,128)S(1)}, f32[128,2048]{1,0:T(8,128)}, u32[]{:S(2)}) copy-start(f32[128,2048]{1,0:T(8,128)} %get-tuple-element.14.ready_in.qi_ref) | copy-start | bytes 3145732
  74.1 8.9 %copy-start.1 = (bf16[128,2048]{1,0:T(8,128)(2,1)S(1)}, bf16[128,2048]{1,0:T(8,128)(2,1)}, u32[]{:S(2)}) copy-start(bf16[128,2048]{1,0:T(8,128)(2,1)} %v_ref.1) | copy-start | bytes 1572868

commit v3 on v1

--- a/solution.py
+++ b/solution.py
@@ -16,6 +16,7 @@
 F32 = jnp.float32
 BF16 = jnp.bfloat16
 GROUP = 4
+AGAIN = 8
 VMEM_LIMIT = 16 * 1024 * 1024
 
 NT = (((1,), (1,)), ((), ()))
@@ -34,6 +35,13 @@
 def swap_halves(x):
     first = (lanes(x.shape[0]) % HD) < HALF
     return jnp.where(first, pltpu.roll(x, PAIR - HALF, 1), pltpu.roll(x, HALF, 1))
+
+
+def swap_matrix():
+    row = lax.broadcasted_iota(jnp.int32, (PAIR, PAIR), 0)
+    lane = lanes(PAIR)
+    source = jnp.where(lane % HD < HALF, lane + HALF, lane - HALF)
+    return jnp.where(row == source, 1.0, 0.0).astype(BF16)
 
 
 def rotated(x, cosine, sine):
@@ -68,53 +76,57 @@
     return pl.ds(pl.multiple_of(first * PAIR, PAIR), count * PAIR)
 
 
+def store(results, sems, first, group):
+    pairs = results[0][0].shape[1] // PAIR
+    at = span(lax.rem(first + group * GROUP, pairs), GROUP)
+    copies = [
+        pltpu.make_async_copy(src.at[:, at], dst.at[:, at], sems.at[group, i])
+        for i, (src, dst) in enumerate(results)
+    ]
+    for copy in copies:
+        copy.start()
+    return copies
+
+
 def states_kernel(
-    pos_ref, q_in, k_in, v_in, g_in,
+    pos_in, q_in, k_in, v_in, g_in,
     qr_ref, kr_ref, v_ref, g_ref, cos_ref, sin_ref, theirs_ref, mine_ref,
-    q_ref, k_ref, sems,
+    pos_ref, q_ref, k_ref, sems, pos_sem,
 ):
     pairs = q_ref.shape[1] // PAIR
-    core = lax.axis_index("core")
-    first = (1 - core) * (pairs // 2)
-    sources = ((q_in, q_ref), (k_in, k_ref), (v_in, v_ref), (g_in, g_ref))
-
-    def copies(group):
-        at = span(lax.rem(first + group * GROUP, pairs), GROUP)
-        return [
-            pltpu.make_async_copy(src.at[:, at], dst.at[:, at], sems.at[group, i])
-            for i, (src, dst) in enumerate(sources)
-        ]
-
-    for group in range(pairs // GROUP):
-        for copy in copies(group):
-            copy.start()
+    first = (1 - lax.axis_index("core")) * (pairs // 2)
+    pos_copy = pltpu.make_async_copy(pos_in, pos_ref, pos_sem)
+    pos_copy.start()
+    arrays = ((q_in, q_ref), (g_in, g_ref), (k_in, k_ref), (v_in, v_ref))
+    copies = [pltpu.make_async_copy(src, dst, sems.at[i]) for i, (src, dst) in enumerate(arrays)]
+    for copy in copies:
+        copy.start()
+    pos_copy.wait()
     cosine, sine = angle_tables(pos_ref[...])
     cos_ref[...] = cosine
     sin_ref[...] = sine
-    for j in range(pairs):
-        if j % GROUP == 0:
-            for copy in copies(j // GROUP):
-                copy.wait()
-        at = span(lax.rem(first + j, pairs))
-        q = rotated(q_ref[:, at], cosine, sine).astype(BF16)
-        k = rotated(k_ref[:, at], cosine, sine).astype(BF16)
-        qr_ref[:, at] = q
-        kr_ref[:, at] = k
-        state = pack_pair(dot(k, v_ref[:, at], TN))
-        grad = pack_pair(dot(q, g_ref[:, at], TN))
-        out, slot = (theirs_ref, 2 * j) if j < pairs // 2 else (mine_ref, 2 * j - pairs)
-        for r in range(2):
-            rows = slice(HALF * r, HALF * (r + 1))
-            out[slot + r, 0] = state[rows].astype(out.dtype)
-            out[slot + r, 1] = grad[rows].astype(out.dtype)
-
-
-def block_kernel(q_ref, k_ref, v_ref, g_ref, qo_ref, ko_ref, vo_ref):
+    swap = swap_matrix()
+    for kind, left, turned, right in ((1, q_ref, qr_ref, g_ref), (0, k_ref, kr_ref, v_ref)):
+        copies[2 - 2 * kind].wait()
+        copies[3 - 2 * kind].wait()
+        for j in range(pairs):
+            at = span(lax.rem(first + j, pairs))
+            x = left[:, at]
+            x = (x.astype(F32) * cosine + dot(x, swap, NN) * sine).astype(BF16)
+            turned[:, at] = x
+            state = pack_pair(dot(x, right[:, at], TN))
+            out, slot = (theirs_ref, 2 * j) if j < pairs // 2 else (mine_ref, 2 * j - pairs)
+            for r in range(2):
+                out[slot + r, kind] = state[HALF * r : HALF * (r + 1)].astype(out.dtype)
+
+
+def block_products(q_ref, k_ref, v_ref, g_ref, qo_ref, ko_ref, vo_ref, again=0):
     row = lax.broadcasted_iota(jnp.int32, (SPAN, 2 * SPAN), 0)
     col = lax.broadcasted_iota(jnp.int32, (SPAN, 2 * SPAN), 1) % SPAN
     lower = row >= col
     upper = row <= col
-    for p in range(q_ref.shape[1] // PAIR):
+    pairs = q_ref.shape[1] // PAIR
+    for p in [*range(again), *range(pairs)]:
         at = slice(p * PAIR, (p + 1) * PAIR)
         q, k, v, g = q_ref[:, at], k_ref[:, at], v_ref[:, at], g_ref[:, at]
         q2, k2, v2, g2 = by_head(q), by_head(k), by_head(v), by_head(g)
@@ -126,10 +138,14 @@
         vo_ref[:, at] = dot(st, g2, NN)
 
 
-def chip_kernel(mine_ref, theirs_ref, out_ref):
-    other = 1 - lax.axis_index("core")
+def chip_kernel(mine_ref, theirs_ref, q_ref, k_ref, v_ref, g_ref, out_ref, qo_ref, ko_ref, vo_ref):
+    core = lax.axis_index("core")
     for z in range(out_ref.shape[0]):
-        out_ref[z] = (mine_ref[z] + theirs_ref[other, z].astype(F32)).astype(BF16)
+        out_ref[z] = (mine_ref[z] + theirs_ref[1 - core, z].astype(F32)).astype(BF16)
+
+    @pl.when(core == 0)
+    def _():
+        block_products(q_ref, k_ref, v_ref, g_ref, qo_ref, ko_ref, vo_ref, AGAIN)
 
 
 def totals_kernel(zr_ref, out_ref):
@@ -159,24 +175,31 @@
         grad += zr_ref[z, 1].astype(F32)
 
 
-def send_kernel(zb_ref, mine_ref, out_ref):
+def send_kernel(
+    zb_ref, mine_ref, q_ref, k_ref, v_ref, g_ref, qi_ref, ki_ref, vi_ref, out_ref, qo_ref, ko_ref, vo_ref
+):
+    del qi_ref, ki_ref, vi_ref
     core = lax.axis_index("core")
     for z in range(zb_ref.shape[0]):
         out_ref[z, 0] = (zb_ref[z, 0].astype(F32) + jnp.where(core == 0, mine_ref[z, 0], 0.0)).astype(BF16)
         out_ref[z, 1] = (zb_ref[z, 1].astype(F32) + jnp.where(core == 1, mine_ref[z, 1], 0.0)).astype(BF16)
 
+    @pl.when(core == 1)
+    def _():
+        block_products(q_ref, k_ref, v_ref, g_ref, qo_ref, ko_ref, vo_ref)
+
 
 def finish_kernel(
-    factor, k_ref, v_ref, g_ref, cos_ref, sin_ref, zb_ref, theirs_ref, sent_ref, qi_ref, ki_ref, vi_ref,
-    q_out, k_out, v_out, qo_ref, ko_ref, vo_ref, sems,
+    factor, k_ref, v_ref, g_ref, qi_ref, ki_ref, vi_ref, cos_ref, sin_ref, zb_ref, theirs_ref, sent_ref,
+    q_out, k_out, v_out, qo_ref, ko_ref, vo_ref, out_sems,
 ):
     pairs = k_ref.shape[1] // PAIR
     core = lax.axis_index("core")
     other = 1 - core
     first = core * (pairs // 2)
+    results = ((qo_ref, q_out), (ko_ref, k_out), (vo_ref, v_out))
     cosine, sine = cos_ref[...], -sin_ref[...]
-    results = ((qo_ref, q_out), (ko_ref, k_out), (vo_ref, v_out))
-    copies = []
+    stores = []
 
     def carried(slot, kind):
         count = zb_ref.shape[0]
@@ -196,12 +219,8 @@
         qo_ref[:, at] = rotated(qo, cosine, sine).astype(BF16)
         ko_ref[:, at] = rotated(ko, cosine, sine).astype(BF16)
         if j % GROUP == GROUP - 1:
-            group = j // GROUP
-            done = span(lax.rem(first + group * GROUP, pairs), GROUP)
-            for i, (src, dst) in enumerate(results):
-                copies.append(pltpu.make_async_copy(src.at[:, done], dst.at[:, done], sems.at[group, i]))
-                copies[-1].start()
-    for copy in copies:
+            stores += store(results, out_sems, first, j // GROUP)
+    for copy in stores:
         copy.wait()
 
 
@@ -209,7 +228,7 @@
 HBM = pl.BlockSpec(memory_space=pltpu.HBM)
 
 
-def call(kernel, out_shape, *args, out_specs=VMEM, in_specs=None, scratch=(), flops=0):
+def call(kernel, out_shape, *args, out_specs=VMEM, in_specs=None, scratch=(), aliases=None):
     in_specs = in_specs or [VMEM] * len(args)
     args = [pltpu.with_memory_space_constraint(x, spec.memory_space) for x, spec in zip(args, in_specs)]
     placed = jax.tree.map(lambda spec, x: spec.memory_space(x.shape, x.dtype), out_specs, out_shape)
@@ -220,7 +239,7 @@
         out_specs=out_specs,
         scratch_shapes=scratch,
         compiler_params=pltpu.CompilerParams(vmem_limit_bytes=VMEM_LIMIT),
-        cost_estimate=pl.CostEstimate(flops=flops, bytes_accessed=2**20, transcendentals=0),
+        input_output_aliases=aliases or {},
     )(*args)
 
 
@@ -241,28 +260,33 @@
         states_kernel,
         [like] * 4 + [table] * 2 + [half_low, half_wide],
         positions.reshape(1, tokens), query_rows, key_rows, value_rows, out_grad,
-        in_specs=[VMEM] + [HBM] * 4,
+        in_specs=[HBM] * 5,
         out_specs=[VMEM] * 8,
-        scratch=[pltpu.VMEM((tokens, width), BF16)] * 2 + [pltpu.SemaphoreType.DMA((groups, 4))],
-    )
+        scratch=[
+            pltpu.VMEM((1, tokens), jnp.int32), pltpu.VMEM((tokens, width), BF16), pltpu.VMEM((tokens, width), BF16),
+            pltpu.SemaphoreType.DMA((4,)), pltpu.SemaphoreType.DMA,
+        ],
+    )
+    rows = (query, key, value, grad)
     theirs = lax.all_gather(theirs, "core")
-    chip = call(chip_kernel, half_low, mine, theirs)
+    chip, *inner = call(chip_kernel, [half_low] + [wide] * 3, mine, theirs, *rows, out_specs=[VMEM] * 4)
     over_z = lax.all_to_all(chip, "z", 0, 0, tiled=True)
-
-    query_in, key_in, value_in = call(
-        block_kernel, [wide] * 3, query, key, value, grad, out_specs=[VMEM] * 3, flops=24 * SPAN**3 * pairs
-    )
-
     group = call(totals_kernel, jax.ShapeDtypeStruct((n_ctx, HALF, PAIR), F32), over_z)
     over_ctx = lax.all_to_all(group, "ctx", 0, 0, tiled=True)
     sums = call(scan_kernel, half_low, over_z, over_ctx)
     back = lax.all_to_all(sums, "z", 0, 0, tiled=True)
-    sent = lax.all_gather(call(send_kernel, half_low, back, mine), "core")
-
+    send, *inner = call(
+        send_kernel,
+        [half_low] + [wide] * 3,
+        back, mine, *rows, *inner,
+        out_specs=[VMEM] * 4,
+        aliases={6: 1, 7: 2, 8: 3},
+    )
+    sent = lax.all_gather(send, "core")
     return call(
         functools.partial(finish_kernel, factor),
         [like] * 3,
-        key, value, grad, cosine, sine, back, theirs, sent, query_in, key_in, value_in,
+        key, value, grad, *inner, cosine, sine, back, theirs, sent,
         out_specs=[HBM] * 3,
         scratch=[pltpu.VMEM((tokens, width), BF16)] * 3 + [pltpu.SemaphoreType.DMA((groups, 3))],
     )

time: 88.4 us -> 80.8 us (0.914)
  blocking collectives: 55 us -> 71.1 us
  starting transfers between devices: 10.2 us -> 0 us
  local copies, waits for them, and re-layouts: 7.9 us -> 0 us
  waiting for transfers between devices: 4.51 us -> 0 us
  Pallas kernels: 9.42 us -> 8.46 us
    all_to_all x0 -> x1, blocking collectives: none -> 18.6 us  [on_device(): back = lax.all_to_all(sums, 'z', 0, 0, tiled=True)]
    all_to_all x1 -> x0, starting transfers between devices: 10.2 us -> none  [on_device(): back = lax.all_to_all(sums, 'z', 0, 0, tiled=True)]
    unnamed x28 -> x0, local copies, waits for them, and re-layouts: 7.9 us -> none
    all_to_all x1 -> x0, waiting for transfers between devices: 4.51 us -> none  [on_device(): back = lax.all_to_all(sums, 'z', 0, 0, tiled=True)]
    all_gather x1, blocking collectives: 8.84 us -> 7.6 us  [on_device(): sent = lax.all_gather(send, 'core')]
    all_to_all x1, blocking collectives: 23.4 us -> 22.1 us  [on_device(): over_z = lax.all_to_all(chip, 'z', 0, 0, tiled=True)]
    pallas_call x7 -> x6, Pallas kernels: 9.42 us -> 8.46 us  [call(): pl.pallas_call(kernel, out_shape=placed, in_specs=in_specs, out_specs=out...]
  transfers between devices with their start and end apart: 1 -> 0, of which waited for: 1 -> 0; matrix products, arithmetic and copies ran while one was open for 0% -> 0% of each run, Pallas kernels for 4% -> 0%
where the time goes in v3:
time: 80.8 us; the launch traced here: 80.2 us
  blocking collectives  71.1 us (88%)
  Pallas kernels  8.46 us (10%)
    all_to_all x1, blocking collectives, on_device(): over_z = lax.all_to_all(chip, 'z', 0, 0, tiled=True)  22.1 us
    all_to_all x1, blocking collectives, on_device(): back = lax.all_to_all(sums, 'z', 0, 0, tiled=True)  18.6 us
    all_to_all x1, blocking collectives, on_device(): over_ctx = lax.all_to_all(group, 'ctx', 0, 0, tiled=True)  14.1 us
    all_gather x1, blocking collectives, on_device(): theirs = lax.all_gather(theirs, 'core')  8.69 us
    pallas_call x6, Pallas kernels, call(): pl.pallas_call(kernel, out_shape=placed, in_specs=in_specs, out_specs=out...  8.46 us
    all_gather x1, blocking collectives, on_device(): sent = lax.all_gather(send, 'core')  7.6 us

profile of v3, /device:TPU:1, one launch (start us, length us, event | category | flops | bytes accessed | tf_op | source)
XLA Modules:
  0.0 80.2 jit_solution(3267537075482947635)
XLA Ops:
  0.6 2.8 %shard_map.76 = (bf16[128,2048]{1,0:T(8,128)(2,1)S(1)}, bf16[128,2048]{1,0:T(8,128)(2,1)S(1)}, bf16[128,2048]{1,0:T(8,128)(2,1)S(1)}, bf16[128,2048]{1,0:T(8,128...) custom-call(s32[1,128]{1,0:T(1,128)} %bitcast.6, ...), custom_call_target="tpu_custom_call" | custom-call | tf_op jit(solution)/shard_map/pallas_call | solution.py:235
  3.4 8.7 %all-gather = bf16[32,2,32,128]{3,2,1,0:T(8,128)(2,1)S(1)} all-gather(bf16[16,2,32,128]{3,2,1,0:T(8,128)(2,1)S(1)} %get-tuple-element.23), channel_id=2, replica_groups=mesh['ctx'=16,'z'=16,'core'=2] {'core'}, dimensions={0}, use_global_device_ids=true | all-gather | bytes 786432 | tf_op jit(solution)/shard_map/all_gather | solution.py:271
  12.2 22.1 %all_to_all.15.zr_ref = bf16[16,2,32,128]{3,2,1,0:T(8,128)(2,1)S(1)} all-to-all(bf16[16,2,32,128]{3,2,1,0:T(8,128)(2,1)S(1)} %get-tuple-element.25), channel_id=1, replica_groups=mesh['ctx'=16,'z'=16,'core'=2] {'z'}, dimensions={0} | all-to-all | bytes 524288 | tf_op jit(solution)/shard_map/all_to_all | solution.py:273
  34.3 0.1 shard_map.78
  34.4 14.1 %all_to_all.16.cx_ref = f32[16,32,128]{2,1,0:T(8,128)S(1)} all-to-all(f32[16,32,128]{2,1,0:T(8,128)S(1)} %shard_map.78), channel_id=1, replica_groups=mesh['ctx'=16,'z'=16,'core'=2] {'ctx'}, dimensions={0} | all-to-all | bytes 524288 | tf_op jit(solution)/shard_map/all_to_all | solution.py:275
  48.5 0.1 shard_map.79
  48.6 18.6 %all_to_all.17.zb_ref = bf16[16,2,32,128]{3,2,1,0:T(8,128)(2,1)S(1)} all-to-all(bf16[16,2,32,128]{3,2,1,0:T(8,128)(2,1)S(1)} %shard_map.79), channel_id=1, replica_groups=mesh['ctx'=16,'z'=16,'core'=2] {'z'}, dimensions={0} | all-to-all | bytes 524288 | tf_op jit(solution)/shard_map/all_to_all | solution.py:277
  67.2 3.2 %shard_map.80 = (bf16[16,2,32,128]{3,2,1,0:T(8,128)(2,1)S(1)}, f32[128,2048]{1,0:T(8,128)S(1)}, f32[128,2048]{1,0:T(8,128)S(1)}, f32[128,2048]{1,0:T(8,128)S(1)}) custom-call(bf16[16,2,32,128]{3,2,1,0:T(8,128)(2,1)S(1)} %all_to_all.17.zb_ref, ...), custom_call_target="tpu_custom_call", output_to_operand_aliasing={{1}: (6, {}), {2}: (7, {}), {3}: (8, {})} | custom-call | tf_op jit(solution)/shard_map/pallas_call | solution.py:235
  70.4 7.6 %all-gather.1 = bf16[32,2,32,128]{3,2,1,0:T(8,128)(2,1)S(1)} all-gather(bf16[16,2,32,128]{3,2,1,0:T(8,128)(2,1)S(1)} %get-tuple-element.34), channel_id=3, replica_groups=mesh['ctx'=16,'z'=16,'core'=2] {'core'}, dimensions={0}, use_global_device_ids=true | all-gather | bytes 786432 | tf_op jit(solution)/shard_map/all_gather | solution.py:285
  78.0 2.3 %shard_map.81 = (bf16[128,2048]{1,0:T(8,128)(2,1)}, bf16[128,2048]{1,0:T(8,128)(2,1)}, bf16[128,2048]{1,0:T(8,128)(2,1)}) custom-call(bf16[128,2048]{1,0:T(8,128)(2,1)S(1)} %get-tuple-element.19.k_ref, bf16[128,2048]{1,0:T(8,128)(2,1)S(1)} %get-tuple-element.20.v_ref, bf16[128,2048]{1,0:T(8,128)(2,1)S(1)} %get-tuple-element.21.g_ref, ...), custom_call_target="tpu_custom_call" | custom-call | tf_op jit(solution)/shard_map/pallas_call | solution.py:235
  (1 shorter events, 0.0 us)

commit v4 on v3

--- a/solution.py
+++ b/solution.py
@@ -16,7 +16,6 @@
 F32 = jnp.float32
 BF16 = jnp.bfloat16
 GROUP = 4
-AGAIN = 8
 VMEM_LIMIT = 16 * 1024 * 1024
 
 NT = (((1,), (1,)), ((), ()))
@@ -45,8 +44,7 @@
 
 
 def rotated(x, cosine, sine):
-    x = x.astype(F32)
-    return x * cosine + swap_halves(x) * sine
+    return x.astype(F32) * cosine + swap_halves(x).astype(F32) * sine
 
 
 def by_head(x):
@@ -61,15 +59,17 @@
 
 
 def angle_tables(positions):
-    lane = lanes(1) % HALF
-    frequency = jnp.ones((1, PAIR), F32)
+    index = lax.broadcasted_iota(jnp.int32, (HALF, positions.shape[1]), 0)
+    frequency = jnp.ones(index.shape, F32)
     for bit in range(HALF.bit_length() - 1):
         part = BASE ** (-(2.0**bit) / HALF)
-        frequency = jnp.where((lane >> bit) % 2 == 1, frequency * part, frequency)
-    tokens = positions.shape[1]
-    angles = jnp.broadcast_to(positions.astype(F32), (tokens, tokens)).T * frequency
-    sign = jnp.where(lanes(1) % HD < HALF, -1.0, 1.0)
-    return jnp.cos(angles), jnp.sin(angles) * sign
+        frequency = jnp.where((index >> bit) % 2 == 1, frequency * part, frequency)
+    angles = positions.astype(F32) * frequency
+    cosine, sine = jnp.cos(angles), jnp.sin(angles)
+    return (
+        jnp.concatenate([cosine, cosine, cosine, cosine], axis=0).T,
+        jnp.concatenate([-sine, sine, -sine, sine], axis=0).T,
+    )
 
 
 def span(first, count=1):
@@ -90,8 +90,8 @@
 
 def states_kernel(
     pos_in, q_in, k_in, v_in, g_in,
-    qr_ref, kr_ref, v_ref, g_ref, cos_ref, sin_ref, theirs_ref, mine_ref,
-    pos_ref, q_ref, k_ref, sems, pos_sem,
+    cos_ref, sin_ref, theirs_ref, mine_ref,
+    pos_ref, q_ref, k_ref, v_ref, g_ref, sems, pos_sem,
 ):
     pairs = q_ref.shape[1] // PAIR
     first = (1 - lax.axis_index("core")) * (pairs // 2)
@@ -106,29 +106,49 @@
     cos_ref[...] = cosine
     sin_ref[...] = sine
     swap = swap_matrix()
-    for kind, left, turned, right in ((1, q_ref, qr_ref, g_ref), (0, k_ref, kr_ref, v_ref)):
+    for kind, left, right in ((1, q_ref, g_ref), (0, k_ref, v_ref)):
         copies[2 - 2 * kind].wait()
         copies[3 - 2 * kind].wait()
         for j in range(pairs):
             at = span(lax.rem(first + j, pairs))
             x = left[:, at]
             x = (x.astype(F32) * cosine + dot(x, swap, NN) * sine).astype(BF16)
-            turned[:, at] = x
             state = pack_pair(dot(x, right[:, at], TN))
             out, slot = (theirs_ref, 2 * j) if j < pairs // 2 else (mine_ref, 2 * j - pairs)
             for r in range(2):
                 out[slot + r, kind] = state[HALF * r : HALF * (r + 1)].astype(out.dtype)
 
 
-def block_products(q_ref, k_ref, v_ref, g_ref, qo_ref, ko_ref, vo_ref, again=0):
+def block_products(
+    q_in, k_in, v_in, g_in, cos_ref, sin_ref, kr_ref, v_ref, g_ref, qo_ref, ko_ref, vo_ref, q_ref, k_ref, sems
+):
+    pairs = q_ref.shape[1] // PAIR
+    arrays = ((q_in, q_ref), (k_in, k_ref), (v_in, v_ref), (g_in, g_ref))
+    copies = []
+    for group in range(pairs // GROUP):
+        at = slice(group * GROUP * PAIR, (group + 1) * GROUP * PAIR)
+        copies.append(
+            [
+                pltpu.make_async_copy(src.at[:, at], dst.at[:, at], sems.at[group, i])
+                for i, (src, dst) in enumerate(arrays)
+            ]
+        )
+        for copy in copies[-1]:
+            copy.start()
+    cosine, sine = cos_ref[...], sin_ref[...]
     row = lax.broadcasted_iota(jnp.int32, (SPAN, 2 * SPAN), 0)
     col = lax.broadcasted_iota(jnp.int32, (SPAN, 2 * SPAN), 1) % SPAN
     lower = row >= col
     upper = row <= col
-    pairs = q_ref.shape[1] // PAIR
-    for p in [*range(again), *range(pairs)]:
+    for p in range(pairs):
+        if p % GROUP == 0:
+            for copy in copies[p // GROUP]:
+                copy.wait()
         at = slice(p * PAIR, (p + 1) * PAIR)
-        q, k, v, g = q_ref[:, at], k_ref[:, at], v_ref[:, at], g_ref[:, at]
+        q = rotated(q_ref[:, at], cosine, sine).astype(BF16)
+        k = rotated(k_ref[:, at], cosine, sine).astype(BF16)
+        v, g = v_ref[:, at], g_ref[:, at]
+        kr_ref[:, at] = k
         q2, k2, v2, g2 = by_head(q), by_head(k), by_head(v), by_head(g)
         w = jnp.where(lower, dot(g, v2, NT), 0.0).astype(BF16)
         wt = jnp.where(upper, dot(v, g2, NT), 0.0).astype(BF16)
@@ -138,14 +158,15 @@
         vo_ref[:, at] = dot(st, g2, NN)
 
 
-def chip_kernel(mine_ref, theirs_ref, q_ref, k_ref, v_ref, g_ref, out_ref, qo_ref, ko_ref, vo_ref):
+def chip_kernel(mine_ref, theirs_ref, *refs):
+    block_in, out_ref, block = refs[:6], refs[6], refs[7:]
     core = lax.axis_index("core")
     for z in range(out_ref.shape[0]):
         out_ref[z] = (mine_ref[z] + theirs_ref[1 - core, z].astype(F32)).astype(BF16)
 
     @pl.when(core == 0)
     def _():
-        block_products(q_ref, k_ref, v_ref, g_ref, qo_ref, ko_ref, vo_ref, AGAIN)
+        block_products(*block_in, *block)
 
 
 def totals_kernel(zr_ref, out_ref):
@@ -156,7 +177,7 @@
         grad += zr_ref[z, 1].astype(F32)
     me = lax.axis_index("ctx")
     for j in range(out_ref.shape[0]):
-        out_ref[j] = jnp.where(j > me, state, grad)
+        out_ref[j] = jnp.where(j > me, state, grad).astype(out_ref.dtype)
 
 
 def scan_kernel(zr_ref, cx_ref, out_ref):
@@ -164,8 +185,8 @@
     state = jnp.zeros(cx_ref.shape[1:], F32)
     grad = jnp.zeros(cx_ref.shape[1:], F32)
     for j in range(cx_ref.shape[0]):
-        state += jnp.where(j < me, cx_ref[j], 0.0)
-        grad += jnp.where(j > me, cx_ref[j], 0.0)
+        state += jnp.where(j < me, cx_ref[j].astype(F32), 0.0)
+        grad += jnp.where(j > me, cx_ref[j].astype(F32), 0.0)
     count = zr_ref.shape[0]
     for z in range(count):
         out_ref[z, 0] = state.astype(BF16)
@@ -175,10 +196,8 @@
         grad += zr_ref[z, 1].astype(F32)
 
 
-def send_kernel(
-    zb_ref, mine_ref, q_ref, k_ref, v_ref, g_ref, qi_ref, ki_ref, vi_ref, out_ref, qo_ref, ko_ref, vo_ref
-):
-    del qi_ref, ki_ref, vi_ref
+def send_kernel(zb_ref, mine_ref, *refs):
+    block_in, out_ref, block = refs[:6], refs[12], refs[13:]
     core = lax.axis_index("core")
     for z in range(zb_ref.shape[0]):
         out_ref[z, 0] = (zb_ref[z, 0].astype(F32) + jnp.where(core == 0, mine_ref[z, 0], 0.0)).astype(BF16)
@@ -186,7 +205,7 @@
 
     @pl.when(core == 1)
     def _():
-        block_products(q_ref, k_ref, v_ref, g_ref, qo_ref, ko_ref, vo_ref)
+        block_products(*block_in, *block)
 
 
 def finish_kernel(
@@ -256,39 +275,50 @@
     half_low = jax.ShapeDtypeStruct((pairs, 2, HALF, PAIR), BF16)
     half_wide = jax.ShapeDtypeStruct((pairs, 2, HALF, PAIR), F32)
 
-    query, key, value, grad, cosine, sine, theirs, mine = call(
+    low = pltpu.VMEM((tokens, width), BF16)
+    rows = (query_rows, key_rows, value_rows, out_grad)
+    cosine, sine, theirs, mine = call(
         states_kernel,
-        [like] * 4 + [table] * 2 + [half_low, half_wide],
-        positions.reshape(1, tokens), query_rows, key_rows, value_rows, out_grad,
+        [table] * 2 + [half_low, half_wide],
+        positions.reshape(1, tokens), *rows,
         in_specs=[HBM] * 5,
-        out_specs=[VMEM] * 8,
-        scratch=[
-            pltpu.VMEM((1, tokens), jnp.int32), pltpu.VMEM((tokens, width), BF16), pltpu.VMEM((tokens, width), BF16),
-            pltpu.SemaphoreType.DMA((4,)), pltpu.SemaphoreType.DMA,
-        ],
-    )
-    rows = (query, key, value, grad)
+        out_specs=[VMEM] * 4,
+        scratch=[pltpu.VMEM((1, tokens), jnp.int32)]
+        + [low] * 4
+        + [pltpu.SemaphoreType.DMA((4,)), pltpu.SemaphoreType.DMA],
+    )
     theirs = lax.all_gather(theirs, "core")
-    chip, *inner = call(chip_kernel, [half_low] + [wide] * 3, mine, theirs, *rows, out_specs=[VMEM] * 4)
+    block = [like] * 3 + [wide] * 3
+    scratch = [low] * 2 + [pltpu.SemaphoreType.DMA((groups, 4))]
+    chip, *inner = call(
+        chip_kernel,
+        [half_low] + block,
+        mine, theirs, *rows, cosine, sine,
+        in_specs=[VMEM] * 2 + [HBM] * 4 + [VMEM] * 2,
+        out_specs=[VMEM] * 7,
+        scratch=scratch,
+    )
     over_z = lax.all_to_all(chip, "z", 0, 0, tiled=True)
-    group = call(totals_kernel, jax.ShapeDtypeStruct((n_ctx, HALF, PAIR), F32), over_z)
+    group = call(totals_kernel, jax.ShapeDtypeStruct((n_ctx, HALF, PAIR), BF16), over_z)
     over_ctx = lax.all_to_all(group, "ctx", 0, 0, tiled=True)
     sums = call(scan_kernel, half_low, over_z, over_ctx)
     back = lax.all_to_all(sums, "z", 0, 0, tiled=True)
     send, *inner = call(
         send_kernel,
-        [half_low] + [wide] * 3,
-        back, mine, *rows, *inner,
-        out_specs=[VMEM] * 4,
-        aliases={6: 1, 7: 2, 8: 3},
+        [half_low] + block,
+        back, mine, *rows, cosine, sine, *inner,
+        in_specs=[VMEM] * 2 + [HBM] * 4 + [VMEM] * 8,
+        out_specs=[VMEM] * 7,
+        scratch=scratch,
+        aliases={8 + i: 1 + i for i in range(6)},
     )
     sent = lax.all_gather(send, "core")
     return call(
         functools.partial(finish_kernel, factor),
         [like] * 3,
-        key, value, grad, *inner, cosine, sine, back, theirs, sent,
+        *inner, cosine, sine, back, theirs, sent,
         out_specs=[HBM] * 3,
-        scratch=[pltpu.VMEM((tokens, width), BF16)] * 3 + [pltpu.SemaphoreType.DMA((groups, 3))],
+        scratch=[low] * 3 + [pltpu.SemaphoreType.DMA((groups, 3))],
     )
 
 

time: 80.8 us -> 80.2 us (level)
  blocking collectives: 71.1 us -> 68.9 us
  Pallas kernels: 8.46 us -> 10.1 us
    pallas_call x6, Pallas kernels: 8.46 us -> 10.1 us  [call(): pl.pallas_call(kernel, out_shape=placed, in_specs=in_specs, out_specs=out...]
    all_gather x1, blocking collectives: 7.6 us -> 6.09 us  [on_device(): sent = lax.all_gather(send, 'core')]
where the time goes in v4:
time: 80.2 us; the launch traced here: 79.7 us
  blocking collectives  68.9 us (86%)
  Pallas kernels  10.1 us (13%)
    all_to_all x1, blocking collectives, on_device(): over_z = lax.all_to_all(chip, 'z', 0, 0, tiled=True)  22.1 us
    all_to_all x1, blocking collectives, on_device(): back = lax.all_to_all(sums, 'z', 0, 0, tiled=True)  18.6 us
    all_to_all x1, blocking collectives, on_device(): over_ctx = lax.all_to_all(group, 'ctx', 0, 0, tiled=True)  13.4 us
    pallas_call x6, Pallas kernels, call(): pl.pallas_call(kernel, out_shape=placed, in_specs=in_specs, out_specs=out...  10.1 us
    all_gather x1, blocking collectives, on_device(): theirs = lax.all_gather(theirs, 'core')  8.68 us
    all_gather x1, blocking collectives, on_device(): sent = lax.all_gather(send, 'core')  6.09 us

profile of v4, /device:TPU:1, one launch (start us, length us, event | category | flops | bytes accessed | tf_op | source)
XLA Modules:
  0.0 79.7 jit_solution(6205246496406038990)
XLA Ops:
  0.6 2.7 %shard_map.76 = (f32[128,128]{1,0:T(8,128)S(1)}, f32[128,128]{1,0:T(8,128)S(1)}, bf16[16,2,32,128]{3,2,1,0:T(8,128)(2,1)S(1)}, f32[16,2,32,128]{3,2,1,0:T(8,128)S(1)}) custom-call(s32[1,128]{1,0:T(1,128)} %bitcast.6, bf16[128,2048]{1,0:T(8,128)(2,1)} %refs_0_.3, bf16[128,2048]{1,0:T(8,128)(2,1)} %refs_1_.3, bf16[128,2048]{1,0:T(8,128)(2,1)} %refs_2_.3, ...), custom_call_target="tpu_custom_call" | custom-call | tf_op jit(solution)/shard_map/pallas_call | solution.py:254
  3.3 8.7 %all-gather = bf16[32,2,32,128]{3,2,1,0:T(8,128)(2,1)S(1)} all-gather(bf16[16,2,32,128]{3,2,1,0:T(8,128)(2,1)S(1)} %get-tuple-element.22), channel_id=2, replica_groups=mesh['ctx'=16,'z'=16,'core'=2] {'core'}, dimensions={0}, use_global_device_ids=true | all-gather | bytes 786432 | tf_op jit(solution)/shard_map/all_gather | solution.py:290
  12.0 0.2 shard_map.77
  12.2 22.1 %all_to_all.15.zr_ref = bf16[16,2,32,128]{3,2,1,0:T(8,128)(2,1)S(1)} all-to-all(bf16[16,2,32,128]{3,2,1,0:T(8,128)(2,1)S(1)} %get-tuple-element.25), channel_id=1, replica_groups=mesh['ctx'=16,'z'=16,'core'=2] {'z'}, dimensions={0} | all-to-all | bytes 524288 | tf_op jit(solution)/shard_map/all_to_all | solution.py:301
  34.4 0.1 shard_map.78
  34.4 13.4 %all_to_all.16.cx_ref = bf16[16,32,128]{2,1,0:T(8,128)(2,1)S(1)} all-to-all(bf16[16,32,128]{2,1,0:T(8,128)(2,1)S(1)} %shard_map.78), channel_id=1, replica_groups=mesh['ctx'=16,'z'=16,'core'=2] {'ctx'}, dimensions={0} | all-to-all | bytes 262144 | tf_op jit(solution)/shard_map/all_to_all | solution.py:303
  47.8 0.1 shard_map.79
  47.9 18.6 %all_to_all.17.zb_ref = bf16[16,2,32,128]{3,2,1,0:T(8,128)(2,1)S(1)} all-to-all(bf16[16,2,32,128]{3,2,1,0:T(8,128)(2,1)S(1)} %shard_map.79), channel_id=1, replica_groups=mesh['ctx'=16,'z'=16,'core'=2] {'z'}, dimensions={0} | all-to-all | bytes 524288 | tf_op jit(solution)/shard_map/all_to_all | solution.py:305
  66.5 4.9 %shard_map.80 = (bf16[16,2,32,128]{3,2,1,0:T(8,128)(2,1)S(1)}, bf16[128,2048]{1,0:T(8,128)(2,1)S(1)}, bf16[128,2048]{1,0:T(8,128)(2,1)S(1)}, bf16[128,2048]{1,0:...) custom-call(bf16[16,2,32,128]{3,2,1,0:T(8,128)(2,1)S(1)} %all_to_all, ...), custom_call_target="tpu_custom_call", output_to_operand_aliasing={{1}: (8, {}), {2}: (9, {}), {3}: (10, {}), {4}: (11, {}), {... | custom-call | tf_op jit(solution)/shard_map/pallas_call | solution.py:254
  71.5 6.1 %all-gather.1 = bf16[32,2,32,128]{3,2,1,0:T(8,128)(2,1)S(1)} all-gather(bf16[16,2,32,128]{3,2,1,0:T(8,128)(2,1)S(1)} %get-tuple-element.38), channel_id=3, replica_groups=mesh['ctx'=16,'z'=16,'core'=2] {'core'}, dimensions={0}, use_global_device_ids=true | all-gather | bytes 786432 | tf_op jit(solution)/shard_map/all_gather | solution.py:315
  77.6 2.1 %shard_map.81 = (bf16[128,2048]{1,0:T(8,128)(2,1)}, bf16[128,2048]{1,0:T(8,128)(2,1)}, bf16[128,2048]{1,0:T(8,128)(2,1)}) custom-call(bf16[128,2048]{1,0:T(8,128)(2,1)S(1)} %get-tuple-element.32.k_ref, bf16[128,2048]{1,0:T(8,128)(2,1)S(1)} %get-tuple-element.33.v_ref, bf16[128,2048]{1,0:T(8,128)(2,1)S(1)} %get-tuple-element.34.g_ref, ...), custom_call_target="tpu_custom_call" | custom-call | tf_op jit(solution)/shard_map/pallas_call | solution.py:254

commit v5 on v4

--- a/solution.py
+++ b/solution.py
@@ -169,6 +169,20 @@
         block_products(*block_in, *block)
 
 
+def z_members(count):
+    middle = count // 2
+    return [middle, middle - 1, *range(middle + 1, count), *range(middle - 2, -1, -1)]
+
+
+def ctx_members(count):
+    side = math.isqrt(count)
+
+    def hops(i):
+        return sum(min(at, side - at) for at in (i // side, i % side))
+
+    return sorted(range(count), key=lambda i: (hops(i), i), reverse=True)
+
+
 def totals_kernel(zr_ref, out_ref):
     state = zr_ref[0, 0].astype(F32)
     grad = zr_ref[0, 1].astype(F32)
@@ -176,24 +190,25 @@
         state += zr_ref[z, 0].astype(F32)
         grad += zr_ref[z, 1].astype(F32)
     me = lax.axis_index("ctx")
-    for j in range(out_ref.shape[0]):
-        out_ref[j] = jnp.where(j > me, state, grad).astype(out_ref.dtype)
+    for slot, j in enumerate(ctx_members(out_ref.shape[0])):
+        out_ref[slot] = jnp.where(j > me, state, grad).astype(out_ref.dtype)
 
 
 def scan_kernel(zr_ref, cx_ref, out_ref):
     me = lax.axis_index("ctx")
     state = jnp.zeros(cx_ref.shape[1:], F32)
     grad = jnp.zeros(cx_ref.shape[1:], F32)
-    for j in range(cx_ref.shape[0]):
-        state += jnp.where(j < me, cx_ref[j].astype(F32), 0.0)
-        grad += jnp.where(j > me, cx_ref[j].astype(F32), 0.0)
-    count = zr_ref.shape[0]
-    for z in range(count):
-        out_ref[z, 0] = state.astype(BF16)
-        state += zr_ref[z, 0].astype(F32)
-    for z in reversed(range(count)):
-        out_ref[z, 1] = grad.astype(BF16)
-        grad += zr_ref[z, 1].astype(F32)
+    for slot, j in enumerate(ctx_members(cx_ref.shape[0])):
+        state += jnp.where(j < me, cx_ref[slot].astype(F32), 0.0)
+        grad += jnp.where(j > me, cx_ref[slot].astype(F32), 0.0)
+    order = z_members(zr_ref.shape[0])
+    slots = [order.index(z) for z in range(len(order))]
+    for at in slots:
+        out_ref[at, 0] = state.astype(BF16)
+        state += zr_ref[at, 0].astype(F32)
+    for at in reversed(slots):
+        out_ref[at, 1] = grad.astype(BF16)
+        grad += zr_ref[at, 1].astype(F32)
 
 
 def send_kernel(zb_ref, mine_ref, *refs):
@@ -298,11 +313,11 @@
         out_specs=[VMEM] * 7,
         scratch=scratch,
     )
-    over_z = lax.all_to_all(chip, "z", 0, 0, tiled=True)
+    over_z = lax.all_to_all(chip, "z", 0, 0, tiled=True, axis_index_groups=[z_members(n_z)])
     group = call(totals_kernel, jax.ShapeDtypeStruct((n_ctx, HALF, PAIR), BF16), over_z)
-    over_ctx = lax.all_to_all(group, "ctx", 0, 0, tiled=True)
+    over_ctx = lax.all_to_all(group, "ctx", 0, 0, tiled=True, axis_index_groups=[ctx_members(n_ctx)])
     sums = call(scan_kernel, half_low, over_z, over_ctx)
-    back = lax.all_to_all(sums, "z", 0, 0, tiled=True)
+    back = lax.all_to_all(sums, "z", 0, 0, tiled=True, axis_index_groups=[z_members(n_z)])
     send, *inner = call(
         send_kernel,
         [half_low] + block,

time: 80.2 us -> 74.1 us (0.924)
  blocking collectives: 68.9 us -> 63.1 us
    all_to_all x3, blocking collectives: 54.1 us -> 48.3 us  [the longest x1 19.9 us: on_device(): lax.all_to_all(chip, 'z', 0, 0, tiled=True, axis_index_groups=[z_members(...]
where the time goes in v5:
time: 74.1 us; the launch traced here: 73.8 us
  blocking collectives  63.1 us (85%)
  Pallas kernels  10.1 us (14%)
    all_to_all x1, blocking collectives, on_device(): lax.all_to_all(chip, 'z', 0, 0, tiled=True, axis_index_groups=[z_members(...  19.9 us
    all_to_all x1, blocking collectives, on_device(): lax.all_to_all(sums, 'z', 0, 0, tiled=True, axis_index_groups=[z_members(...  18.3 us
    all_to_all x1, blocking collectives, on_device(): lax.all_to_all(group, 'ctx', 0, 0, tiled=True, axis_index_groups=[ctx_mem...  10.1 us
    pallas_call x6, Pallas kernels, call(): pl.pallas_call(kernel, out_shape=placed, in_specs=in_specs, out_specs=out...  10.1 us
    all_gather x1, blocking collectives, on_device(): theirs = lax.all_gather(theirs, 'core')  8.68 us
    all_gather x1, blocking collectives, on_device(): sent = lax.all_gather(send, 'core')  6.06 us

profile of v5, /device:TPU:1, one launch (start us, length us, event | category | flops | bytes accessed | tf_op | source)
XLA Modules:
  0.0 73.8 jit_solution(10747616578091985069)
XLA Ops:
  0.6 2.7 %shard_map.76 = (f32[128,128]{1,0:T(8,128)S(1)}, f32[128,128]{1,0:T(8,128)S(1)}, bf16[16,2,32,128]{3,2,1,0:T(8,128)(2,1)S(1)}, f32[16,2,32,128]{3,2,1,0:T(8,128)S(1)}) custom-call(s32[1,128]{1,0:T(1,128)} %bitcast.6, bf16[128,2048]{1,0:T(8,128)(2,1)} %refs_0_.3, bf16[128,2048]{1,0:T(8,128)(2,1)} %refs_1_.3, bf16[128,2048]{1,0:T(8,128)(2,1)} %refs_2_.3, ...), custom_call_target="tpu_custom_call" | custom-call | tf_op jit(solution)/shard_map/pallas_call | solution.py:269
  3.3 8.7 %all-gather = bf16[32,2,32,128]{3,2,1,0:T(8,128)(2,1)S(1)} all-gather(bf16[16,2,32,128]{3,2,1,0:T(8,128)(2,1)S(1)} %get-tuple-element.22), channel_id=2, replica_groups=mesh['ctx'=16,'z'=16,'core'=2] {'core'}, dimensions={0}, use_global_device_ids=true | all-gather | bytes 786432 | tf_op jit(solution)/shard_map/all_gather | solution.py:305
  12.0 0.2 shard_map.77
  12.2 19.9 %all_to_all.15.zr_ref = bf16[16,2,32,128]{3,2,1,0:T(8,128)(2,1)S(1)} all-to-all(bf16[16,2,32,128]{3,2,1,0:T(8,128)(2,1)S(1)} %get-tuple-element.25), channel_id=1, replica_groups={{16,14,18,20,22,24,26,28,30,12,10,8,6,4,2,0},{17,15,19,21,23,25,27,29,3..., dimensions={0} | all-to-all | bytes 524288 | tf_op jit(solution)/shard_map/all_to_all | solution.py:316
  32.1 0.1 shard_map.78
  32.2 10.1 %all_to_all.16.cx_ref = bf16[16,32,128]{2,1,0:T(8,128)(2,1)S(1)} all-to-all(bf16[16,32,128]{2,1,0:T(8,128)(2,1)S(1)} %shard_map.78), channel_id=1, replica_groups={{320,448,352,288,192,480,416,256,224,160,64,384,128,96,32,0},{321,449,3..., dimensions={0} | all-to-all | bytes 262144 | tf_op jit(solution)/shard_map/all_to_all | solution.py:318
  42.3 0.1 shard_map.79
  42.4 18.3 %all_to_all.17.zb_ref = bf16[16,2,32,128]{3,2,1,0:T(8,128)(2,1)S(1)} all-to-all(bf16[16,2,32,128]{3,2,1,0:T(8,128)(2,1)S(1)} %shard_map.79), channel_id=1, replica_groups={{16,14,18,20,22,24,26,28,30,12,10,8,6,4,2,0},{17,15,19,21,23,25,27,29,3..., dimensions={0} | all-to-all | bytes 524288 | tf_op jit(solution)/shard_map/all_to_all | solution.py:320
  60.7 4.9 %shard_map.80 = (bf16[16,2,32,128]{3,2,1,0:T(8,128)(2,1)S(1)}, bf16[128,2048]{1,0:T(8,128)(2,1)S(1)}, bf16[128,2048]{1,0:T(8,128)(2,1)S(1)}, bf16[128,2048]{1,0:...) custom-call(bf16[16,2,32,128]{3,2,1,0:T(8,128)(2,1)S(1)} %all_to_all, ...), custom_call_target="tpu_custom_call", output_to_operand_aliasing={{1}: (8, {}), {2}: (9, {}), {3}: (10, {}), {4}: (11, {}), {... | custom-call | tf_op jit(solution)/shard_map/pallas_call | solution.py:269
  65.7 6.1 %all-gather.1 = bf16[32,2,32,128]{3,2,1,0:T(8,128)(2,1)S(1)} all-gather(bf16[16,2,32,128]{3,2,1,0:T(8,128)(2,1)S(1)} %get-tuple-element.38), channel_id=3, replica_groups=mesh['ctx'=16,'z'=16,'core'=2] {'core'}, dimensions={0}, use_global_device_ids=true | all-gather | bytes 786432 | tf_op jit(solution)/shard_map/all_gather | solution.py:330
  71.7 2.1 %shard_map.81 = (bf16[128,2048]{1,0:T(8,128)(2,1)}, bf16[128,2048]{1,0:T(8,128)(2,1)}, bf16[128,2048]{1,0:T(8,128)(2,1)}) custom-call(bf16[128,2048]{1,0:T(8,128)(2,1)S(1)} %get-tuple-element.32.k_ref, bf16[128,2048]{1,0:T(8,128)(2,1)S(1)} %get-tuple-element.33.v_ref, bf16[128,2048]{1,0:T(8,128)(2,1)S(1)} %get-tuple-element.34.g_ref, ...), custom_call_target="tpu_custom_call" | custom-call | tf_op jit(solution)/shard_map/pallas_call | solution.py:269

commit v6 on v5

--- a/solution.py
+++ b/solution.py
@@ -180,7 +180,7 @@
     def hops(i):
         return sum(min(at, side - at) for at in (i // side, i % side))
 
-    return sorted(range(count), key=lambda i: (hops(i), i), reverse=True)
+    return sorted(range(count), key=lambda i: (hops(i), i % side, i), reverse=True)
 
 
 def totals_kernel(zr_ref, out_ref):

time: 74.1 us -> 74.2 us (level)
  no operation moved by 1% of the time
where the time goes in v6:
time: 74.2 us; the launch traced here: 73.9 us
  blocking collectives  63.1 us (85%)
  Pallas kernels  10.1 us (14%)
    all_to_all x1, blocking collectives, on_device(): lax.all_to_all(chip, 'z', 0, 0, tiled=True, axis_index_groups=[z_members(...  19.9 us
    all_to_all x1, blocking collectives, on_device(): lax.all_to_all(sums, 'z', 0, 0, tiled=True, axis_index_groups=[z_members(...  18.3 us
    all_to_all x1, blocking collectives, on_device(): lax.all_to_all(group, 'ctx', 0, 0, tiled=True, axis_index_groups=[ctx_mem...  10.1 us
    pallas_call x6, Pallas kernels, call(): pl.pallas_call(kernel, out_shape=placed, in_specs=in_specs, out_specs=out...  10.1 us
    all_gather x1, blocking collectives, on_device(): theirs = lax.all_gather(theirs, 'core')  8.68 us
    all_gather x1, blocking collectives, on_device(): sent = lax.all_gather(send, 'core')  6.11 us

profile of v6, /device:TPU:1, one launch (start us, length us, event | category | flops | bytes accessed | tf_op | source)
XLA Modules:
  0.0 73.9 jit_solution(6932848403078445577)
XLA Ops:
  0.6 2.7 %shard_map.76 = (f32[128,128]{1,0:T(8,128)S(1)}, f32[128,128]{1,0:T(8,128)S(1)}, bf16[16,2,32,128]{3,2,1,0:T(8,128)(2,1)S(1)}, f32[16,2,32,128]{3,2,1,0:T(8,128)S(1)}) custom-call(s32[1,128]{1,0:T(1,128)} %bitcast.6, bf16[128,2048]{1,0:T(8,128)(2,1)} %refs_0_.3, bf16[128,2048]{1,0:T(8,128)(2,1)} %refs_1_.3, bf16[128,2048]{1,0:T(8,128)(2,1)} %refs_2_.3, ...), custom_call_target="tpu_custom_call" | custom-call | tf_op jit(solution)/shard_map/pallas_call | solution.py:269
  3.3 8.7 %all-gather = bf16[32,2,32,128]{3,2,1,0:T(8,128)(2,1)S(1)} all-gather(bf16[16,2,32,128]{3,2,1,0:T(8,128)(2,1)S(1)} %get-tuple-element.22), channel_id=2, replica_groups=mesh['ctx'=16,'z'=16,'core'=2] {'core'}, dimensions={0}, use_global_device_ids=true | all-gather | bytes 786432 | tf_op jit(solution)/shard_map/all_gather | solution.py:305
  12.0 0.2 shard_map.77
  12.2 19.9 %all_to_all.15.zr_ref = bf16[16,2,32,128]{3,2,1,0:T(8,128)(2,1)S(1)} all-to-all(bf16[16,2,32,128]{3,2,1,0:T(8,128)(2,1)S(1)} %get-tuple-element.25), channel_id=1, replica_groups={{16,14,18,20,22,24,26,28,30,12,10,8,6,4,2,0},{17,15,19,21,23,25,27,29,3..., dimensions={0} | all-to-all | bytes 524288 | tf_op jit(solution)/shard_map/all_to_all | solution.py:316
  32.1 0.1 shard_map.78
  32.2 10.1 %all_to_all.16.cx_ref = bf16[16,32,128]{2,1,0:T(8,128)(2,1)S(1)} all-to-all(bf16[16,32,128]{2,1,0:T(8,128)(2,1)S(1)} %shard_map.78), channel_id=1, replica_groups={{320,352,448,192,288,480,224,64,416,160,256,96,32,384,128,0},{321,353,4..., dimensions={0} | all-to-all | bytes 262144 | tf_op jit(solution)/shard_map/all_to_all | solution.py:318
  42.3 0.1 shard_map.79
  42.4 18.3 %all_to_all.17.zb_ref = bf16[16,2,32,128]{3,2,1,0:T(8,128)(2,1)S(1)} all-to-all(bf16[16,2,32,128]{3,2,1,0:T(8,128)(2,1)S(1)} %shard_map.79), channel_id=1, replica_groups={{16,14,18,20,22,24,26,28,30,12,10,8,6,4,2,0},{17,15,19,21,23,25,27,29,3..., dimensions={0} | all-to-all | bytes 524288 | tf_op jit(solution)/shard_map/all_to_all | solution.py:320
  60.7 4.9 %shard_map.80 = (bf16[16,2,32,128]{3,2,1,0:T(8,128)(2,1)S(1)}, bf16[128,2048]{1,0:T(8,128)(2,1)S(1)}, bf16[128,2048]{1,0:T(8,128)(2,1)S(1)}, bf16[128,2048]{1,0:...) custom-call(bf16[16,2,32,128]{3,2,1,0:T(8,128)(2,1)S(1)} %all_to_all, ...), custom_call_target="tpu_custom_call", output_to_operand_aliasing={{1}: (8, {}), {2}: (9, {}), {3}: (10, {}), {4}: (11, {}), {... | custom-call | tf_op jit(solution)/shard_map/pallas_call | solution.py:269
  65.7 6.1 %all-gather.1 = bf16[32,2,32,128]{3,2,1,0:T(8,128)(2,1)S(1)} all-gather(bf16[16,2,32,128]{3,2,1,0:T(8,128)(2,1)S(1)} %get-tuple-element.38), channel_id=3, replica_groups=mesh['ctx'=16,'z'=16,'core'=2] {'core'}, dimensions={0}, use_global_device_ids=true | all-gather | bytes 786432 | tf_op jit(solution)/shard_map/all_gather | solution.py:330
  71.8 2.1 %shard_map.81 = (bf16[128,2048]{1,0:T(8,128)(2,1)}, bf16[128,2048]{1,0:T(8,128)(2,1)}, bf16[128,2048]{1,0:T(8,128)(2,1)}) custom-call(bf16[128,2048]{1,0:T(8,128)(2,1)S(1)} %get-tuple-element.32.k_ref, bf16[128,2048]{1,0:T(8,128)(2,1)S(1)} %get-tuple-element.33.v_ref, bf16[128,2048]{1,0:T(8,128)(2,1)S(1)} %get-tuple-element.34.g_ref, ...), custom_call_target="tpu_custom_call" | custom-call | tf_op jit(solution)/shard_map/pallas_call | solution.py:269
